TPU v7x, 256 devices: a whole 4x4x8 slice. The times are simulated.
256 devices in a mesh: gx: 32 (over z, x), gy: 8 (over y, core).
Axes of the slice: x: 4, y: 4, z: 8, core: 2. Of those that a mesh axis runs over, the one named last changes fastest.
Arguments:
- density: float32 [128, 64, 256], P('gx', 'gy'), may hold values from 0.3 to 1
- passive_void_mask: int32 [128, 64, 256], P('gx', 'gy'), may hold values 0 or 1
- support_node_mask: int32 [128, 64, 256], P('gx', 'gy'), may hold values 0 or 1
- loaded_node_mask: int32 [2, 128, 64, 256], P(None, 'gx', 'gy'), may hold values 0 or 1
- traction: float32 [2, 3, 128, 64, 256], P(None, None, 'gx', 'gy'), may hold values from -6 to 6
Outputs:
- displacement: float32 [2, 3, 128, 64, 256], P(None, None, 'gx', 'gy')
- sensitivity: float32 [128, 64, 256], P('gx', 'gy')
- compliance: float32 [2], replicated
All inputs are finite; a program needn't handle non-finite values. No bound on the sum of `passive_void_mask` or of `support_node_mask` or of `loaded_node_mask` on one device may be relied on, other than what follows from the above.
Results may differ from a plain program's by a relative error of at most 0.0003.
Values sent between devices are 32-bit elements; how exact they have to be, the bound alone decides.
A program may use at most 64 MiB of HBM per device.

v0:
```python
import math

import jax
import jax.numpy as jnp
import numpy as np
from jax import lax
from jax.sharding import PartitionSpec as P

LEVELS = 3
SWEEPS = 4


damping = 0.5
stiff_min = 0.001
penalty = 3.0
sharpness = 8.0
threshold = 0.5
filter_radius = 3.0
corner_list = [
    (0, 0, 0),
    (0, 0, 1),
    (0, 1, 0),
    (0, 1, 1),
    (1, 0, 0),
    (1, 0, 1),
    (1, 1, 0),
    (1, 1, 1),
]


def passed_along(shard, axis, by):
    devices = lax.axis_size(axis)
    pairs = [(i, i + by) for i in range(devices) if 0 <= i + by < devices]
    return lax.ppermute(shard, axis, pairs)


def padded_2(block, sides, width):
    for axis, dim in sides:
        count = lax.axis_size(axis)
        forward = [(i, i + 1) for i in range(count - 1)]
        backward = [(target, source) for source, target in forward]
        low = lax.ppermute(
            lax.slice_in_dim(block, block.shape[dim] - width, None, axis=dim), axis, forward
        )
        high = lax.ppermute(lax.slice_in_dim(block, 0, width, axis=dim), axis, backward)
        block = jnp.concatenate([low, block, high], axis=dim)
    return block


def element_stiffness():
    poisson = 0.3
    lame_first = poisson / ((1.0 + poisson) * (1.0 - 2.0 * poisson))
    lame_shear = 1.0 / (2.0 * (1.0 + poisson))
    elastic = np.zeros((6, 6))
    elastic[:3, :3] = lame_first
    for number in range(3):
        elastic[number, number] = lame_first + 2.0 * lame_shear
        elastic[number + 3, number + 3] = lame_shear
    points = [0.5 - 0.5 / math.sqrt(3.0), 0.5 + 0.5 / math.sqrt(3.0)]
    matrix = np.zeros((24, 24))
    for point_x in points:
        for point_y in points:
            for point_z in points:
                where_at = (point_x, point_y, point_z)
                strain = np.zeros((6, 24))
                for number, corner in enumerate(corner_list):
                    slopes = []
                    for direction in range(3):
                        factor = 1.0
                        for second in range(3):
                            if second == direction:
                                factor = factor * (1.0 if corner[second] else -1.0)
                            elif corner[second]:
                                factor = factor * where_at[second]
                            else:
                                factor = factor * (1.0 - where_at[second])
                        slopes.append(factor)
                    column = 3 * number
                    strain[0, column] = slopes[0]
                    strain[1, column + 1] = slopes[1]
                    strain[2, column + 2] = slopes[2]
                    strain[3, column] = slopes[1]
                    strain[3, column + 1] = slopes[0]
                    strain[4, column + 1] = slopes[2]
                    strain[4, column + 2] = slopes[1]
                    strain[5, column] = slopes[2]
                    strain[5, column + 2] = slopes[0]
                matrix = matrix + strain.T @ elastic @ strain / 8.0
    return matrix.reshape(8, 3, 8, 3).astype(np.float32)


def filter_offsets():
    entries = []
    for offset_x in range(-2, 3):
        for offset_y in range(-2, 3):
            for offset_z in range(-2, 3):
                weight = filter_radius - math.sqrt(
                    offset_x * offset_x + offset_y * offset_y + offset_z * offset_z
                )
                if weight > 0.0:
                    entries.append((offset_x, offset_y, offset_z, weight))
    return entries


def weighted_sum(padded, begin, counts):
    running = jnp.zeros(counts, jnp.float32)
    for offset_x, offset_y, offset_z, weight in filter_offsets():
        start_x = begin[0] + offset_x
        start_y = begin[1] + offset_y
        start_z = begin[2] + offset_z
        running = (
            running
            + weight
            * padded[
                start_x : start_x + counts[0],
                start_y : start_y + counts[1],
                start_z : start_z + counts[2],
            ]
        )
    return running


def projection(filtered):
    edge_value = jnp.tanh(sharpness * threshold)
    total_range = edge_value + jnp.tanh(sharpness * (1.0 - threshold))
    level_value = jnp.tanh(sharpness * (filtered - threshold))
    return (
        (edge_value + level_value) / total_range,
        sharpness * (1.0 - level_value * level_value) / total_range,
    )


def element_apply(field_pad, stiff_pad, scale_factor, wanted):
    element_table = jnp.asarray(element_stiffness())
    count_x = field_pad.shape[2] - 2
    count_y = field_pad.shape[3] - 2
    count_z = field_pad.shape[4] - 2
    results = []
    energies = []
    for load_index in range(field_pad.shape[0]):
        stacked = jnp.stack(
            [
                field_pad[
                    load_index,
                    :,
                    step_x : step_x + count_x + 1,
                    step_y : step_y + count_y + 1,
                    step_z : step_z + count_z + 1,
                ]
                for step_x, step_y, step_z in corner_list
            ]
        )
        forces = jnp.einsum(
            "acbd,bdxyz->acxyz", element_table, stacked, precision=lax.Precision.HIGHEST
        )
        if wanted != "energy":
            weighted = forces * (scale_factor * stiff_pad)
            running = jnp.zeros((3, count_x, count_y, count_z), jnp.float32)
            for number, (step_x, step_y, step_z) in enumerate(corner_list):
                running = (
                    running
                    + weighted[
                        number,
                        :,
                        1 - step_x : 1 - step_x + count_x,
                        1 - step_y : 1 - step_y + count_y,
                        1 - step_z : 1 - step_z + count_z,
                    ]
                )
            results.append(running)
        if wanted != "result":
            energies.append(
                jnp.sum(stacked[:, :, 1:, 1:, 1:] * forces[:, :, 1:, 1:, 1:], axis=(0, 1))
            )
    result = jnp.stack(results) if results else None
    energy = jnp.stack(energies) if energies else None
    return (result, energy)


def node_diagonal(stiff_pad, scale_factor):
    count_x = stiff_pad.shape[0] - 1
    count_y = stiff_pad.shape[1] - 1
    count_z = stiff_pad.shape[2] - 1
    running = jnp.zeros((count_x, count_y, count_z), jnp.float32)
    for step_x, step_y, step_z in corner_list:
        running = (
            running
            + stiff_pad[
                1 - step_x : 1 - step_x + count_x,
                1 - step_y : 1 - step_y + count_y,
                1 - step_z : 1 - step_z + count_z,
            ]
        )
    return float(element_stiffness()[0, 0, 0, 0]) * scale_factor * running


def coarsen(stiffness):
    count_x, count_y, count_z = stiffness.shape
    return jnp.mean(
        stiffness.reshape(count_x // 2, 2, count_y // 2, 2, count_z // 2, 2), axis=(1, 3, 5)
    )


def restrict_axis(values, dimension):
    length = values.shape[dimension] - 1
    even_rows = lax.slice_in_dim(values, 0, length, 2, dimension)
    middle = lax.slice_in_dim(values, 1, length + 1, 2, dimension)
    upper_rows = lax.slice_in_dim(values, 2, length + 1, 2, dimension)
    return 0.5 * even_rows + middle + 0.5 * upper_rows


def prolong_axis(values, dimension):
    count_rows = values.shape[dimension] - 1
    lesser = lax.slice_in_dim(values, 0, count_rows, 1, dimension)
    higher = lax.slice_in_dim(values, 1, count_rows + 1, 1, dimension)
    paired = jnp.stack([lesser, 0.5 * (lesser + higher)], axis=dimension + 1)
    new_shape = list(lesser.shape)
    new_shape[dimension] = 2 * count_rows
    return paired.reshape(new_shape)


def extend(values, by):
    if by > 0:
        face_y = values[..., -1:, :]
    else:
        face_y = values[..., :1, :]
    arrived = passed_along(face_y, "gy", by)
    if by > 0:
        values = jnp.concatenate([arrived, values], axis=-2)
        face_x = values[..., -1:, :, :]
    else:
        values = jnp.concatenate([values, arrived], axis=-2)
        face_x = values[..., :1, :, :]
    arrived = passed_along(face_x, "gx", by)
    if by > 0:
        return jnp.concatenate([arrived, values], axis=-3)
    return jnp.concatenate([values, arrived], axis=-3)


def lower_pad(stiffness):
    return jnp.pad(extend(stiffness, 1), ((0, 0), (0, 0), (1, 0)))


def apply_level(field, stiff_pad, scale_factor, wanted):
    padded = padded_2(field, (("gx", 2), ("gy", 3)), 1)
    padded = jnp.pad(padded, ((0, 0), (0, 0), (0, 0), (0, 0), (1, 1)))
    return element_apply(padded, stiff_pad, scale_factor, wanted)


def axis_inside(position, axis_count, count_rows, width):
    place = position * count_rows + jnp.arange(-width, count_rows + width, dtype=jnp.int32)
    return jnp.where((place >= 0) & (place < count_rows * axis_count), 1.0, 0.0).astype(jnp.float32)


def padded_inside(width, count_x, count_y, count_z):
    inside_x = axis_inside(lax.axis_index("gx"), lax.axis_size("gx"), count_x, width)
    inside_y = axis_inside(lax.axis_index("gy"), lax.axis_size("gy"), count_y, width)
    inside_z = jnp.pad(jnp.ones((count_z,), jnp.float32), 2)
    return inside_x[:, None, None] * inside_y[None, :, None] * inside_z[None, None, :]


def cycle(level_index, right_side, pads, stiffs, diags, keep_node):
    scale_factor = 2.0**level_index
    if level_index == LEVELS - 1:
        approx = damping * right_side / diags[level_index]
        for sweep_index in range(SWEEPS - 1):
            image = apply_level(approx, pads[level_index], scale_factor, "result")[0]
            approx = approx + damping * (right_side - image) / diags[level_index]
        return approx
    approx = damping * right_side / diags[level_index]
    image = apply_level(approx, pads[level_index], scale_factor, "result")[0]
    if level_index == 0:
        image = keep_node * image
    coarse = jnp.pad(extend(right_side - image, 1), ((0, 0), (0, 0), (0, 0), (0, 0), (1, 0)))
    for dimension in (2, 3, 4):
        coarse = restrict_axis(coarse, dimension)
    correction = cycle(level_index + 1, coarse, pads, stiffs, diags, keep_node)
    correction = jnp.pad(extend(correction, -1), ((0, 0), (0, 0), (0, 0), (0, 0), (0, 1)))
    for dimension in (2, 3, 4):
        correction = prolong_axis(correction, dimension)
    if level_index == 0:
        correction = keep_node * correction
    approx = approx + correction
    image = apply_level(approx, pads[level_index], scale_factor, "result")[0]
    if level_index == 0:
        image = keep_node * image
    return approx + damping * (right_side - image) / diags[level_index]


def per_device(density, passive_void_mask, support_node_mask, loaded_node_mask, traction):
    size_x, size_y, size_z = density.shape
    keep_elem = 1.0 - passive_void_mask.astype(jnp.float32)
    grown_rim = padded_2(density, (("gx", 0), ("gy", 1)), 2)
    grown_rim = jnp.pad(grown_rim, ((0, 0), (0, 0), (2, 2)))
    inside = padded_inside(2, size_x, size_y, size_z)
    numerator = weighted_sum(grown_rim, (2, 2, 2), (size_x, size_y, size_z))
    denominator = weighted_sum(inside, (2, 2, 2), (size_x, size_y, size_z))
    shaped, slope_value = projection(numerator / denominator)
    physical = keep_elem * shaped
    stiffness = stiff_min + (1.0 - stiff_min) * physical**penalty
    first_pad = lower_pad(stiffness)
    stiffs = [stiffness]
    pads = [first_pad]
    for level_index in range(1, LEVELS):
        stiffs.append(coarsen(stiffs[-1]))
        pads.append(lower_pad(stiffs[-1]))
    diags = [node_diagonal(pads[level_index], 2.0**level_index) for level_index in range(LEVELS)]
    keep_node = 1.0 - support_node_mask.astype(jnp.float32)
    right_side = keep_node * (loaded_node_mask.astype(jnp.float32)[:, None] * traction)
    precond = cycle(0, right_side, pads, stiffs, diags, keep_node)
    local_dot = jnp.sum(right_side * precond, axis=(1, 2, 3, 4))
    preconditioned_inner_product = lax.psum(local_dot, ("gx", "gy"))
    image = apply_level(precond, pads[0], 1.0, "result")[0]
    image = keep_node * image
    local_curve = jnp.sum(precond * image, axis=(1, 2, 3, 4))
    curvature = lax.psum(local_curve, ("gx", "gy"))
    conjugate_step_size = preconditioned_inner_product / curvature
    displacement = conjugate_step_size[:, None, None, None, None] * precond
    total_cells = size_x * size_y * size_z * lax.axis_size("gx") * lax.axis_size("gy")
    compliance = conjugate_step_size * preconditioned_inner_product / total_cells
    energy = apply_level(displacement, pads[0], 1.0, "energy")[1]
    energy_total = jnp.sum(energy, axis=0)
    ratio_field = (
        -energy_total
        * penalty
        * physical ** (penalty - 1.0)
        * (1.0 - stiff_min)
        * keep_elem
        * slope_value
        / denominator
    )
    spread = padded_2(ratio_field, (("gx", 0), ("gy", 1)), 2)
    spread = jnp.pad(spread, ((0, 0), (0, 0), (2, 2)))
    sensitivity = weighted_sum(spread, (2, 2, 2), (size_x, size_y, size_z))
    return (displacement, sensitivity, compliance)


def solution(mesh):
    in_specs = (
        P("gx", "gy", None),
        P("gx", "gy", None),
        P("gx", "gy", None),
        P(None, "gx", "gy", None),
        P(None, None, "gx", "gy", None),
    )
    out_specs = (P(None, None, "gx", "gy", None), P("gx", "gy", None), P())
    return jax.shard_map(
        per_device, mesh=mesh, in_specs=in_specs, out_specs=out_specs, check_vma=False
    )
```

profile of v0, /device:TPU:103, one launch (start us, length us, event | category | flops | bytes accessed | tf_op | source)
XLA Modules:
  0.0 493.7 jit_solution(12819529274012268632)
XLA Ops:
  3.8 6.1 %collective-permute-start = (f32[2,8,256]{2,1,0:T(8,128)S(1)}, f32[2,8,256]{2,1,0:T(8,128)S(1)}, u32[]{:S(2)}, u32[]{:S(2)}) collective-permute-start(f32[2,8,256]{2,1,0:T(8,128)S(1)} %get-tuple-element.209), channel_id=1, source_target_pairs={{0,8},{8,16},{16,24},{24,32},{32,40},{40,48},{48,56},{56,64},{64,7... | collective-permute-start | bytes 49160 | tf_op jit(solution)/shard_map/ppermute | solution.py:42
  11.6 4.9 collective-permute-start.2
  28.9 7.2 %collective-permute-start.5 = (f32[1,9,256]{2,1,0:T(8,128)S(1)}, f32[1,9,256]{2,1,0:T(8,128)S(1)}, u32[]{:S(2)}, u32[]{:S(2)}) collective-permute-start(f32[1,9,256]{2,1,0:T(8,128)S(1)} %pad_maximum_fusion.30), channel_id=1, source_target_pairs={{0,8},{8,16},{16,24},{24,32},{32,40},{40,48},{48,56},{56,64},{64,7... | collective-permute-start | bytes 27656 | tf_op jit(solution)/shard_map/ppermute | solution.py:34
  36.1 3.9 collective-permute-start.12
  40.7 3.7 collective-permute-start.6
  46.3 5.0 %collective-permute-start.20 = (f32[1,1,64]{2,1,0:T(1,128)S(1)}, f32[1,1,64]{2,1,0:T(1,128)S(1)}, u32[]{:S(2)}, u32[]{:S(2)}) collective-permute-start(f32[1,1,64]{2,1,0:T(1,128)S(1)} %slice.2399), channel_id=1, source_target_pairs={{0,1},{1,2},{2,3},{3,4},{4,5},{5,6},{6,7},{8,9},{9,10},{10,11},{11... | collective-permute-start | bytes 776 | tf_op jit(solution)/shard_map/ppermute | solution.py:34
  52.5 6.2 %collective-permute-start.8 = (f32[2,3,6,1,256]{4,0,1,3,2:T(2,128)S(1)}, f32[2,3,6,1,256]{4,0,1,3,2:T(2,128)S(1)}, u32[]{:S(2)}, u32[]{:S(2)}) collective-permute-start(f32[2,3,6,1,256]{4,0,1,3,2:T(2,128)S(1)} %get-tuple-element.97), channel_id=1, source_target_pairs={{0,1},{1,2},{2,3},{3,4},{4,5},{5,6},{6,7},{8,9},{9,10},{10,11},{11... | collective-permute-start | bytes 110600 | tf_op jit(solution)/shard_map/ppermute | solution.py:42
  64.6 6.3 %fusion.445 = (f32[1,3,5,9,257]{4,0,1,3,2:T(1,128)}, f32[1,3,5,9,257]{4,0,1,3,2:T(1,128)S(1)}, f32[1,3,5,9,257]{4,0,1,3,2:T(1,128)S(1)}, f32[1,3,5,9,257]{4,0,1,...) fusion(f32[2,3,6,10,258]{4,0,1,3,2:T(2,128)S(1)} %select_maximu, ...), kind=kLoop, calls=%fused_computation.1026 | loop fusion | bytes 4440960 | tf_op jit(solution)/shard_map/slice | solution.py:143
  70.9 5.7 %stack.151 = f32[8,3,5,9,257]{4,0,1,3,2:T(8,128)S(1)} concatenate(f32[1,3,5,9,257]{4,0,1,3,2:T(1,128)} %get-tuple-element.89, f32[1,3,5,9,257]{4,0,1,3,2:T(1,128)} %get-tuple-element.88, f32[1,3,5,9,257]{4,0,1,3,2:T(1,128)} %get-tuple-element.87, f32[1,3,5,9,257]{4,0,1,3,2:T(1,128)} %get-tuple-element.86, f32[1,3,5,9,257]{4,0,1,3,2:T(1,128)} %get-tuple-element.85, ...), dimensions={0} | concatenate | bytes 2220480 | tf_op jit(solution)/shard_map/stack | solution.py:141
  79.3 5.5 %stack.152 = f32[8,3,5,9,257]{4,0,1,3,2:T(8,128)S(1)} concatenate(f32[1,3,5,9,257]{4,0,1,3,2:T(1,128)} %get-tuple-element.82, f32[1,3,5,9,257]{4,0,1,3,2:T(1,128)S(1)} %get-tuple-element.81, f32[1,3,5,9,257]{4,0,1,3,2:T(1,128)S(1)} %get-tuple-element.80, f32[1,3,5,9,257]{4,0,1,3,2:T(1,128)S(1)} %get-tuple-element.79, f32[1,3,5,9,257]{4,0,1,3,2:T(1,128)S(1)} %get-tuple-element.78, ...), dimensions={0} | concatenate | bytes 2220480 | tf_op jit(solution)/shard_map/stack | solution.py:141
  86.4 5.7 %slice_add_fusion.30 = (f32[1,3,4,8,256]{4,0,1,3,2:T(1,128)S(1)}, f32[1,3,4,8,256]{4,0,1,3,2:T(1,128)S(1)}) fusion(f32[8,3,5,9,257]{4,0,1,3,2:T(8,128)S(1)} %fusion.20, f32[8,3,5,9,257]{4,0,1,3,2:T(8,128)} %fusion.21), kind=kLoop, calls=%fused_computation.199 | loop fusion | flops 344064 | bytes 1769472 | tf_op jit(solution)/shard_map/add | solution.py:161
  98.0 3.9 collective-permute-done.11
  108.2 5.0 %collective-permute-start.14 = (f32[2,3,1,4,128]{4,0,1,3,2:T(2,128)S(1)}, f32[2,3,1,4,128]{4,0,1,3,2:T(2,128)S(1)}, u32[]{:S(2)}, u32[]{:S(2)}) collective-permute-start(f32[2,3,1,4,128]{4,0,1,3,2:T(2,128)S(1)} %get-tuple-element.214), channel_id=1, source_target_pairs={{0,8},{8,16},{16,24},{24,32},{32,40},{40,48},{48,56},{56,64},{64,7... | collective-permute-start | bytes 36872 | tf_op jit(solution)/shard_map/ppermute | solution.py:42
  115.2 6.7 %collective-permute-start.21 = (f32[1,3,64]{2,1,0:T(4,128)S(1)}, f32[1,3,64]{2,1,0:T(4,128)S(1)}, u32[]{:S(2)}, u32[]{:S(2)}) collective-permute-start(f32[1,3,64]{2,1,0:T(4,128)S(1)} %pad_maximum_fusion.41), channel_id=1, source_target_pairs={{0,8},{8,16},{16,24},{24,32},{32,40},{40,48},{48,56},{56,64},{64,7... | collective-permute-start | bytes 2312 | tf_op jit(solution)/shard_map/ppermute | solution.py:34
  121.9 5.2 %collective-permute-start.16 = (f32[2,3,4,1,128]{4,0,1,3,2:T(2,128)S(1)}, f32[2,3,4,1,128]{4,0,1,3,2:T(2,128)S(1)}, u32[]{:S(2)}, u32[]{:S(2)}) collective-permute-start(f32[2,3,4,1,128]{4,0,1,3,2:T(2,128)S(1)} %get-tuple-element.153), channel_id=1, source_target_pairs={{0,1},{1,2},{2,3},{3,4},{4,5},{5,6},{6,7},{8,9},{9,10},{10,11},{11... | collective-permute-start | bytes 36872 | tf_op jit(solution)/shard_map/ppermute | solution.py:42
  147.2 6.7 %collective-permute-start.22 = (f32[2,3,1,2,64]{4,0,1,3,2:T(2,128)S(1)}, f32[2,3,1,2,64]{4,0,1,3,2:T(2,128)S(1)}, u32[]{:S(2)}, u32[]{:S(2)}) collective-permute-start(f32[2,3,1,2,64]{4,0,1,3,2:T(2,128)S(1)} %get-tuple-element.20), channel_id=1, source_target_pairs={{0,8},{8,16},{16,24},{24,32},{32,40},{40,48},{48,56},{56,64},{64,7... | collective-permute-start | bytes 9224 | tf_op jit(solution)/shard_map/ppermute | solution.py:42
  154.7 6.1 %collective-permute-start.24 = (f32[2,3,3,1,64]{4,0,1,3,2:T(2,128)S(1)}, f32[2,3,3,1,64]{4,0,1,3,2:T(2,128)S(1)}, u32[]{:S(2)}, u32[]{:S(2)}) collective-permute-start(f32[2,3,3,1,64]{4,0,1,3,2:T(2,128)S(1)} %get-tuple-element.224), channel_id=1, source_target_pairs={{0,1},{1,2},{2,3},{3,4},{4,5},{5,6},{6,7},{8,9},{9,10},{10,11},{11... | collective-permute-start | bytes 13832 | tf_op jit(solution)/shard_map/ppermute | solution.py:42
  169.0 7.2 %collective-permute-start.26 = (f32[2,3,1,2,64]{4,0,1,3,2:T(2,128)S(1)}, f32[2,3,1,2,64]{4,0,1,3,2:T(2,128)S(1)}, u32[]{:S(2)}, u32[]{:S(2)}) collective-permute-start(f32[2,3,1,2,64]{4,0,1,3,2:T(2,128)S(1)} %divide_add_fusion.4), channel_id=1, source_target_pairs={{0,8},{8,16},{16,24},{24,32},{32,40},{40,48},{48,56},{56,64},{64,7... | collective-permute-start | bytes 9224 | tf_op jit(solution)/shard_map/ppermute | solution.py:42
  188.1 7.2 %collective-permute-start.30 = (f32[2,3,1,2,64]{4,0,1,3,2:T(2,128)S(1)}, f32[2,3,1,2,64]{4,0,1,3,2:T(2,128)S(1)}, u32[]{:S(2)}, u32[]{:S(2)}) collective-permute-start(f32[2,3,1,2,64]{4,0,1,3,2:T(2,128)S(1)} %divide_add_fusion.3), channel_id=1, source_target_pairs={{0,8},{8,16},{16,24},{24,32},{32,40},{40,48},{48,56},{56,64},{64,7... | collective-permute-start | bytes 9224 | tf_op jit(solution)/shard_map/ppermute | solution.py:42
  212.1 6.3 %collective-permute-done.35 = f32[2,3,1,3,64]{4,0,1,3,2:T(2,128)S(1)} collective-permute-done((f32[2,3,1,3,64]{4,0,1,3,2:T(2,128)S(1)}, f32[2,3,1,3,64]{4,0,1,3,2:T(2,128)S(1)}, u32[]{:S(2)}, u32[]{:S(2)}) %collective-permute-start.35) | collective-permute-done | bytes 4640 | tf_op jit(solution)/shard_map/ppermute | solution.py:34
  219.6 3.4 collective-permute-start.36
  224.9 6.2 %collective-permute-done.37 = f32[2,3,1,4,128]{4,0,1,3,2:T(2,128)S(1)} collective-permute-done((f32[2,3,1,4,128]{4,0,1,3,2:T(2,128)S(1)}, f32[2,3,1,4,128]{4,0,1,3,2:T(2,128)S(1)}, u32[]{:S(2)}, u32[]{:S(2)}) %collective-permute-start.37) | collective-permute-done | bytes 12320 | tf_op jit(solution)/shard_map/ppermute | solution.py:45
  231.1 4.1 collective-permute-start.38
  251.6 5.7 %collective-permute-done.41 = f32[2,3,1,5,128]{4,0,1,3,2:T(2,128)S(1)} collective-permute-done((f32[2,3,1,5,128]{4,0,1,3,2:T(2,128)S(1)}, f32[2,3,1,5,128]{4,0,1,3,2:T(2,128)S(1)}, u32[]{:S(2)}, u32[]{:S(2)}) %collective-permute-start.41) | collective-permute-done | bytes 15392 | tf_op jit(solution)/shard_map/ppermute | solution.py:34
  258.6 3.3 copy.45
  266.8 3.4 collective-permute-start.43
  270.2 5.1 %collective-permute-done.43 = f32[2,3,1,8,256]{4,0,1,3,2:T(2,128)S(1)} collective-permute-done((f32[2,3,1,8,256]{4,0,1,3,2:T(2,128)S(1)}, f32[2,3,1,8,256]{4,0,1,3,2:T(2,128)S(1)}, u32[]{:S(2)}, u32[]{:S(2)}) %collective-permute-start.43) | collective-permute-done | bytes 49184 | tf_op jit(solution)/shard_map/ppermute | solution.py:45
  275.3 4.0 collective-permute-start.44
  281.2 3.3 collective-permute-done.45
  285.2 6.3 %fusion.444 = (f32[1,3,5,9,257]{4,0,1,3,2:T(1,128)}, f32[1,3,5,9,257]{4,0,1,3,2:T(1,128)S(1)}, f32[1,3,5,9,257]{4,0,1,3,2:T(1,128)S(1)}, f32[1,3,5,9,257]{4,0,1,...) fusion(f32[2,3,6,10,258]{4,0,1,3,2:T(2,128)S(1)} %select_maximu, ...), kind=kLoop, calls=%fused_computation.1025 | loop fusion | bytes 4440960 | tf_op jit(solution)/shard_map/slice | solution.py:143
  291.5 5.7 %stack.187 = f32[8,3,5,9,257]{4,0,1,3,2:T(8,128)S(1)} concatenate(f32[1,3,5,9,257]{4,0,1,3,2:T(1,128)} %get-tuple-element.73, f32[1,3,5,9,257]{4,0,1,3,2:T(1,128)} %get-tuple-element.72, f32[1,3,5,9,257]{4,0,1,3,2:T(1,128)} %get-tuple-element.71, f32[1,3,5,9,257]{4,0,1,3,2:T(1,128)} %get-tuple-element.70, f32[1,3,5,9,257]{4,0,1,3,2:T(1,128)} %get-tuple-element.69, ...), dimensions={0} | concatenate | bytes 2220480 | tf_op jit(solution)/shard_map/stack | solution.py:141
  300.3 5.5 %stack.188 = f32[8,3,5,9,257]{4,0,1,3,2:T(8,128)S(1)} concatenate(f32[1,3,5,9,257]{4,0,1,3,2:T(1,128)} %get-tuple-element.66, f32[1,3,5,9,257]{4,0,1,3,2:T(1,128)S(1)} %get-tuple-element.65, f32[1,3,5,9,257]{4,0,1,3,2:T(1,128)S(1)} %get-tuple-element.64, f32[1,3,5,9,257]{4,0,1,3,2:T(1,128)S(1)} %get-tuple-element.63, f32[1,3,5,9,257]{4,0,1,3,2:T(1,128)S(1)} %get-tuple-element.62, ...), dimensions={0} | concatenate | bytes 2220480 | tf_op jit(solution)/shard_map/stack | solution.py:141
  310.7 3.4 collective-permute-start.47
  314.1 4.8 collective-permute-done.47
  328.1 6.3 %fusion.443 = (f32[1,3,5,9,257]{4,0,1,3,2:T(1,128)}, f32[1,3,5,9,257]{4,0,1,3,2:T(1,128)S(1)}, f32[1,3,5,9,257]{4,0,1,3,2:T(1,128)S(1)}, f32[1,3,5,9,257]{4,0,1,...) fusion(f32[2,3,6,10,258]{4,0,1,3,2:T(2,128)S(1)} %select_maximu, ...), kind=kLoop, calls=%fused_computation.1024 | loop fusion | bytes 4440960 | tf_op jit(solution)/shard_map/slice | solution.py:143
  334.4 5.6 %stack.190 = f32[8,3,5,9,257]{4,0,1,3,2:T(8,128)S(1)} concatenate(f32[1,3,5,9,257]{4,0,1,3,2:T(1,128)} %get-tuple-element.57, f32[1,3,5,9,257]{4,0,1,3,2:T(1,128)} %get-tuple-element.56, f32[1,3,5,9,257]{4,0,1,3,2:T(1,128)} %get-tuple-element.55, f32[1,3,5,9,257]{4,0,1,3,2:T(1,128)} %get-tuple-element.54, f32[1,3,5,9,257]{4,0,1,3,2:T(1,128)} %get-tuple-element.53, ...), dimensions={0} | concatenate | bytes 2220480 | tf_op jit(solution)/shard_map/stack | solution.py:141
  342.5 5.5 %stack.191 = f32[8,3,5,9,257]{4,0,1,3,2:T(8,128)S(1)} concatenate(f32[1,3,5,9,257]{4,0,1,3,2:T(1,128)} %get-tuple-element.50, f32[1,3,5,9,257]{4,0,1,3,2:T(1,128)} %get-tuple-element.49, f32[1,3,5,9,257]{4,0,1,3,2:T(1,128)S(1)} %get-tuple-element.48, f32[1,3,5,9,257]{4,0,1,3,2:T(1,128)S(1)} %get-tuple-element.47, f32[1,3,5,9,257]{4,0,1,3,2:T(1,128)S(1)} %get-tuple-element.46, ...), dimensions={0} | concatenate | bytes 2220480 | tf_op jit(solution)/shard_map/stack | solution.py:141
  351.0 72.2 %all-reduce.19 = (f32[2]{0:T(128)S(1)}, f32[2]{0:T(128)S(1)}) all-reduce(f32[2]{0:T(128)S(1)} %get-tuple-element.13, f32[2]{0:T(128)S(1)} %get-tuple-element.12), channel_id=1, replica_groups=mesh['gx'=32,'gy'=8] {'gx','gy'}, use_global_device_ids=true, to_apply=%region_4.5 | all-reduce | flops 4 | bytes 32 | tf_op jit(solution)/shard_map/psum | solution.py:312
  423.9 5.5 %collective-permute-start.50 = (f32[2,3,1,8,256]{4,0,1,3,2:T(2,128)S(1)}, f32[2,3,1,8,256]{4,0,1,3,2:T(2,128)S(1)}, u32[]{:S(2)}, u32[]{:S(2)}) collective-permute-start(f32[2,3,1,8,256]{4,0,1,3,2:T(2,128)S(1)} %get-tuple-element.99), channel_id=1, source_target_pairs={{0,8},{8,16},{16,24},{24,32},{32,40},{40,48},{48,56},{56,64},{64,7... | collective-permute-start | bytes 147464 | tf_op jit(solution)/shard_map/ppermute | solution.py:42
  431.3 6.2 %collective-permute-done.51 = f32[2,3,1,8,256]{4,0,1,3,2:T(2,128)S(1)} collective-permute-done((f32[2,3,1,8,256]{4,0,1,3,2:T(2,128)S(1)}, f32[2,3,1,8,256]{4,0,1,3,2:T(2,128)S(1)}, u32[]{:S(2)}, u32[]{:S(2)}) %collective-permute-start.51) | collective-permute-done | bytes 49184 | tf_op jit(solution)/shard_map/ppermute | solution.py:45
  437.6 4.4 collective-permute-start.52
  447.9 6.4 %fusion.442 = (f32[1,3,5,9,257]{4,0,1,3,2:T(1,128)S(1)}, f32[1,3,5,9,257]{4,0,1,3,2:T(1,128)S(1)}, f32[1,3,5,9,257]{4,0,1,3,2:T(1,128)S(1)}, f32[1,3,5,9,257]{4,...) fusion(f32[2,3,6,10,258]{4,0,1,3,2:T(2,128)S(1)} %select_maximu, ...), kind=kLoop, calls=%fused_computation.1023 | loop fusion | bytes 4440960 | tf_op jit(solution)/shard_map/slice | solution.py:143
  454.3 5.6 %stack.193 = f32[8,3,5,9,257]{4,0,1,3,2:T(8,128)S(1)} concatenate(f32[1,3,5,9,257]{4,0,1,3,2:T(1,128)} %get-tuple-element.42, f32[1,3,5,9,257]{4,0,1,3,2:T(1,128)} %get-tuple-element.41, f32[1,3,5,9,257]{4,0,1,3,2:T(1,128)} %get-tuple-element.40, f32[1,3,5,9,257]{4,0,1,3,2:T(1,128)} %get-tuple-element.39, f32[1,3,5,9,257]{4,0,1,3,2:T(1,128)} %get-tuple-element.38, ...), dimensions={0} | concatenate | bytes 2220480 | tf_op jit(solution)/shard_map/stack | solution.py:141
  460.0 4.0 fusion.34
  464.4 5.0 %stack.194 = f32[8,3,5,9,257]{4,0,1,3,2:T(8,128)S(1)} concatenate(f32[1,3,5,9,257]{4,0,1,3,2:T(1,128)} %get-tuple-element.34, f32[1,3,5,9,257]{4,0,1,3,2:T(1,128)S(1)} %get-tuple-element.33, f32[1,3,5,9,257]{4,0,1,3,2:T(1,128)S(1)} %get-tuple-element.32, f32[1,3,5,9,257]{4,0,1,3,2:T(1,128)S(1)} %get-tuple-element.31, f32[1,3,5,9,257]{4,0,1,3,2:T(1,128)S(1)} %get-tuple-element.30, ...), dimensions={0} | concatenate | bytes 2220480 | tf_op jit(solution)/shard_map/stack | solution.py:141
  469.5 4.0 fusion.37
  476.0 3.4 collective-permute-start.55
  479.4 4.4 collective-permute-done.55
  (281 shorter events, 173.9 us)
Async XLA Ops:
  1.4 10.2 %collective-permute-start.1 = (f32[2,8,256]{2,1,0:T(8,128)S(1)}, f32[2,8,256]{2,1,0:T(8,128)S(1)}, u32[]{:S(2)}, u32[]{:S(2)}) collective-permute-start(f32[2,8,256]{2,1,0:T(8,128)S(1)} %get-tuple-element.208), channel_id=1, source_target_pairs={{8,0},{16,8},{24,16},{32,24},{40,32},{48,40},{56,48},{64,56},{72,6... | collective-permute-start | bytes 49160 | tf_op jit(solution)/shard_map/ppermute | solution.py:45
  3.8 7.0 %collective-permute-start = (f32[2,8,256]{2,1,0:T(8,128)S(1)}, f32[2,8,256]{2,1,0:T(8,128)S(1)}, u32[]{:S(2)}, u32[]{:S(2)}) collective-permute-start(f32[2,8,256]{2,1,0:T(8,128)S(1)} %get-tuple-element.209), channel_id=1, source_target_pairs={{0,8},{8,16},{16,24},{24,32},{32,40},{40,48},{48,56},{56,64},{64,7... | collective-permute-start | bytes 49160 | tf_op jit(solution)/shard_map/ppermute | solution.py:42
  11.6 6.9 %collective-permute-start.2 = (f32[8,2,256]{2,1,0:T(2,128)S(1)}, f32[8,2,256]{2,1,0:T(2,128)S(1)}, u32[]{:S(2)}, u32[]{:S(2)}) collective-permute-start(f32[8,2,256]{2,1,0:T(2,128)S(1)} %get-tuple-element.149), channel_id=1, source_target_pairs={{0,1},{1,2},{2,3},{3,4},{4,5},{5,6},{6,7},{8,9},{9,10},{10,11},{11... | collective-permute-start | bytes 49160 | tf_op jit(solution)/shard_map/ppermute | solution.py:42
  16.5 5.1 %collective-permute-start.3 = (f32[8,2,256]{2,1,0:T(2,128)S(1)}, f32[8,2,256]{2,1,0:T(2,128)S(1)}, u32[]{:S(2)}, u32[]{:S(2)}) collective-permute-start(f32[8,2,256]{2,1,0:T(2,128)S(1)} %get-tuple-element.150), channel_id=1, source_target_pairs={{1,0},{2,1},{3,2},{4,3},{5,4},{6,5},{7,6},{9,8},{10,9},{11,10},{12... | collective-permute-start | bytes 49160 | tf_op jit(solution)/shard_map/ppermute | solution.py:45
  28.9 11.4 %collective-permute-start.5 = (f32[1,9,256]{2,1,0:T(8,128)S(1)}, f32[1,9,256]{2,1,0:T(8,128)S(1)}, u32[]{:S(2)}, u32[]{:S(2)}) collective-permute-start(f32[1,9,256]{2,1,0:T(8,128)S(1)} %pad_maximum_fusion.30), channel_id=1, source_target_pairs={{0,8},{8,16},{16,24},{24,32},{32,40},{40,48},{48,56},{56,64},{64,7... | collective-permute-start | bytes 27656 | tf_op jit(solution)/shard_map/ppermute | solution.py:34
  36.1 24.5 %collective-permute-start.12 = (f32[2,1,128]{2,1,0:T(1,128)S(1)}, f32[2,1,128]{2,1,0:T(1,128)S(1)}, u32[]{:S(2)}, u32[]{:S(2)}) collective-permute-start(f32[2,1,128]{2,1,0:T(1,128)S(1)} %slice.2993), channel_id=1, source_target_pairs={{0,1},{1,2},{2,3},{3,4},{4,5},{5,6},{6,7},{8,9},{9,10},{10,11},{11... | collective-permute-start | bytes 3080 | tf_op jit(solution)/shard_map/ppermute | solution.py:34
  40.7 10.6 %collective-permute-start.6 = (f32[2,3,1,8,256]{4,0,1,3,2:T(2,128)S(1)}, f32[2,3,1,8,256]{4,0,1,3,2:T(2,128)S(1)}, u32[]{:S(2)}, u32[]{:S(2)}) collective-permute-start(f32[2,3,1,8,256]{4,0,1,3,2:T(2,128)S(1)} %get-tuple-element.107), channel_id=1, source_target_pairs={{0,8},{8,16},{16,24},{24,32},{32,40},{40,48},{48,56},{56,64},{64,7... | collective-permute-start | bytes 147464 | tf_op jit(solution)/shard_map/ppermute | solution.py:42
  44.3 8.2 %collective-permute-start.7 = (f32[2,3,1,8,256]{4,0,1,3,2:T(2,128)S(1)}, f32[2,3,1,8,256]{4,0,1,3,2:T(2,128)S(1)}, u32[]{:S(2)}, u32[]{:S(2)}) collective-permute-start(f32[2,3,1,8,256]{4,0,1,3,2:T(2,128)S(1)} %get-tuple-element.108), channel_id=1, source_target_pairs={{8,0},{16,8},{24,16},{32,24},{40,32},{48,40},{56,48},{64,56},{72,6... | collective-permute-start | bytes 147464 | tf_op jit(solution)/shard_map/ppermute | solution.py:45
  46.3 68.8 %collective-permute-start.20 = (f32[1,1,64]{2,1,0:T(1,128)S(1)}, f32[1,1,64]{2,1,0:T(1,128)S(1)}, u32[]{:S(2)}, u32[]{:S(2)}) collective-permute-start(f32[1,1,64]{2,1,0:T(1,128)S(1)} %slice.2399), channel_id=1, source_target_pairs={{0,1},{1,2},{2,3},{3,4},{4,5},{5,6},{6,7},{8,9},{9,10},{10,11},{11... | collective-permute-start | bytes 776 | tf_op jit(solution)/shard_map/ppermute | solution.py:34
  52.5 10.5 %collective-permute-start.8 = (f32[2,3,6,1,256]{4,0,1,3,2:T(2,128)S(1)}, f32[2,3,6,1,256]{4,0,1,3,2:T(2,128)S(1)}, u32[]{:S(2)}, u32[]{:S(2)}) collective-permute-start(f32[2,3,6,1,256]{4,0,1,3,2:T(2,128)S(1)} %get-tuple-element.97), channel_id=1, source_target_pairs={{0,1},{1,2},{2,3},{3,4},{4,5},{5,6},{6,7},{8,9},{9,10},{10,11},{11... | collective-permute-start | bytes 110600 | tf_op jit(solution)/shard_map/ppermute | solution.py:42
  58.7 5.3 %collective-permute-start.9 = (f32[2,3,6,1,256]{4,0,1,3,2:T(2,128)S(1)}, f32[2,3,6,1,256]{4,0,1,3,2:T(2,128)S(1)}, u32[]{:S(2)}, u32[]{:S(2)}) collective-permute-start(f32[2,3,6,1,256]{4,0,1,3,2:T(2,128)S(1)} %get-tuple-element.98), channel_id=1, source_target_pairs={{1,0},{2,1},{3,2},{4,3},{5,4},{6,5},{7,6},{9,8},{10,9},{11,10},{12... | collective-permute-start | bytes 110600 | tf_op jit(solution)/shard_map/ppermute | solution.py:45
  60.6 34.4 %collective-permute-start.13 = (f32[1,5,128]{2,1,0:T(8,128)S(1)}, f32[1,5,128]{2,1,0:T(8,128)S(1)}, u32[]{:S(2)}, u32[]{:S(2)}) collective-permute-start(f32[1,5,128]{2,1,0:T(8,128)S(1)} %fusion.423), channel_id=1, source_target_pairs={{0,8},{8,16},{16,24},{24,32},{32,40},{40,48},{48,56},{56,64},{64,7... | collective-permute-start | bytes 7688 | tf_op jit(solution)/shard_map/ppermute | solution.py:34
  96.0 5.9 %collective-permute-start.11 = (f32[2,3,1,9,256]{4,0,1,3,2:T(2,128)S(1)}, f32[2,3,1,9,256]{4,0,1,3,2:T(2,128)S(1)}, u32[]{:S(2)}, u32[]{:S(2)}) collective-permute-start(f32[2,3,1,9,256]{4,0,1,3,2:T(2,128)S(1)} %pad_maximum_fusion.4), channel_id=1, source_target_pairs={{0,8},{8,16},{16,24},{24,32},{32,40},{40,48},{48,56},{56,64},{64,7... | collective-permute-start | bytes 165896 | tf_op jit(solution)/shard_map/ppermute | solution.py:34
  108.2 13.6 %collective-permute-start.14 = (f32[2,3,1,4,128]{4,0,1,3,2:T(2,128)S(1)}, f32[2,3,1,4,128]{4,0,1,3,2:T(2,128)S(1)}, u32[]{:S(2)}, u32[]{:S(2)}) collective-permute-start(f32[2,3,1,4,128]{4,0,1,3,2:T(2,128)S(1)} %get-tuple-element.214), channel_id=1, source_target_pairs={{0,8},{8,16},{16,24},{24,32},{32,40},{40,48},{48,56},{56,64},{64,7... | collective-permute-start | bytes 36872 | tf_op jit(solution)/shard_map/ppermute | solution.py:42
  113.2 8.7 %collective-permute-start.15 = (f32[2,3,1,4,128]{4,0,1,3,2:T(2,128)S(1)}, f32[2,3,1,4,128]{4,0,1,3,2:T(2,128)S(1)}, u32[]{:S(2)}, u32[]{:S(2)}) collective-permute-start(f32[2,3,1,4,128]{4,0,1,3,2:T(2,128)S(1)} %get-tuple-element.215), channel_id=1, source_target_pairs={{8,0},{16,8},{24,16},{32,24},{40,32},{48,40},{56,48},{64,56},{72,6... | collective-permute-start | bytes 36872 | tf_op jit(solution)/shard_map/ppermute | solution.py:45
  115.2 23.2 %collective-permute-start.21 = (f32[1,3,64]{2,1,0:T(4,128)S(1)}, f32[1,3,64]{2,1,0:T(4,128)S(1)}, u32[]{:S(2)}, u32[]{:S(2)}) collective-permute-start(f32[1,3,64]{2,1,0:T(4,128)S(1)} %pad_maximum_fusion.41), channel_id=1, source_target_pairs={{0,8},{8,16},{16,24},{24,32},{32,40},{40,48},{48,56},{56,64},{64,7... | collective-permute-start | bytes 2312 | tf_op jit(solution)/shard_map/ppermute | solution.py:34
  121.9 7.6 %collective-permute-start.16 = (f32[2,3,4,1,128]{4,0,1,3,2:T(2,128)S(1)}, f32[2,3,4,1,128]{4,0,1,3,2:T(2,128)S(1)}, u32[]{:S(2)}, u32[]{:S(2)}) collective-permute-start(f32[2,3,4,1,128]{4,0,1,3,2:T(2,128)S(1)} %get-tuple-element.153), channel_id=1, source_target_pairs={{0,1},{1,2},{2,3},{3,4},{4,5},{5,6},{6,7},{8,9},{9,10},{10,11},{11... | collective-permute-start | bytes 36872 | tf_op jit(solution)/shard_map/ppermute | solution.py:42
  127.1 5.0 %collective-permute-start.17 = (f32[2,3,4,1,128]{4,0,1,3,2:T(2,128)S(1)}, f32[2,3,4,1,128]{4,0,1,3,2:T(2,128)S(1)}, u32[]{:S(2)}, u32[]{:S(2)}) collective-permute-start(f32[2,3,4,1,128]{4,0,1,3,2:T(2,128)S(1)} %get-tuple-element.154), channel_id=1, source_target_pairs={{1,0},{2,1},{3,2},{4,3},{5,4},{6,5},{7,6},{9,8},{10,9},{11,10},{12... | collective-permute-start | bytes 36872 | tf_op jit(solution)/shard_map/ppermute | solution.py:45
  145.3 8.6 %collective-permute-start.23 = (f32[2,3,1,2,64]{4,0,1,3,2:T(2,128)S(1)}, f32[2,3,1,2,64]{4,0,1,3,2:T(2,128)S(1)}, u32[]{:S(2)}, u32[]{:S(2)}) collective-permute-start(f32[2,3,1,2,64]{4,0,1,3,2:T(2,128)S(1)} %get-tuple-element.20), channel_id=1, source_target_pairs={{8,0},{16,8},{24,16},{32,24},{40,32},{48,40},{56,48},{64,56},{72,6... | collective-permute-start | bytes 9224 | tf_op jit(solution)/shard_map/ppermute | solution.py:45
  147.2 7.4 %collective-permute-start.22 = (f32[2,3,1,2,64]{4,0,1,3,2:T(2,128)S(1)}, f32[2,3,1,2,64]{4,0,1,3,2:T(2,128)S(1)}, u32[]{:S(2)}, u32[]{:S(2)}) collective-permute-start(f32[2,3,1,2,64]{4,0,1,3,2:T(2,128)S(1)} %get-tuple-element.20), channel_id=1, source_target_pairs={{0,8},{8,16},{16,24},{24,32},{32,40},{40,48},{48,56},{56,64},{64,7... | collective-permute-start | bytes 9224 | tf_op jit(solution)/shard_map/ppermute | solution.py:42
  154.7 8.0 %collective-permute-start.24 = (f32[2,3,3,1,64]{4,0,1,3,2:T(2,128)S(1)}, f32[2,3,3,1,64]{4,0,1,3,2:T(2,128)S(1)}, u32[]{:S(2)}, u32[]{:S(2)}) collective-permute-start(f32[2,3,3,1,64]{4,0,1,3,2:T(2,128)S(1)} %get-tuple-element.224), channel_id=1, source_target_pairs={{0,1},{1,2},{2,3},{3,4},{4,5},{5,6},{6,7},{8,9},{9,10},{10,11},{11... | collective-permute-start | bytes 13832 | tf_op jit(solution)/shard_map/ppermute | solution.py:42
  160.8 5.0 %collective-permute-start.25 = (f32[2,3,3,1,64]{4,0,1,3,2:T(2,128)S(1)}, f32[2,3,3,1,64]{4,0,1,3,2:T(2,128)S(1)}, u32[]{:S(2)}, u32[]{:S(2)}) collective-permute-start(f32[2,3,3,1,64]{4,0,1,3,2:T(2,128)S(1)} %get-tuple-element.225), channel_id=1, source_target_pairs={{1,0},{2,1},{3,2},{4,3},{5,4},{6,5},{7,6},{9,8},{10,9},{11,10},{12... | collective-permute-start | bytes 13832 | tf_op jit(solution)/shard_map/ppermute | solution.py:45
  167.1 9.2 %collective-permute-start.27 = (f32[2,3,1,2,64]{4,0,1,3,2:T(2,128)S(1)}, f32[2,3,1,2,64]{4,0,1,3,2:T(2,128)S(1)}, u32[]{:S(2)}, u32[]{:S(2)}) collective-permute-start(f32[2,3,1,2,64]{4,0,1,3,2:T(2,128)S(1)} %divide_add_fusion.4), channel_id=1, source_target_pairs={{8,0},{16,8},{24,16},{32,24},{40,32},{48,40},{56,48},{64,56},{72,6... | collective-permute-start | bytes 9224 | tf_op jit(solution)/shard_map/ppermute | solution.py:45
  169.0 8.0 %collective-permute-start.26 = (f32[2,3,1,2,64]{4,0,1,3,2:T(2,128)S(1)}, f32[2,3,1,2,64]{4,0,1,3,2:T(2,128)S(1)}, u32[]{:S(2)}, u32[]{:S(2)}) collective-permute-start(f32[2,3,1,2,64]{4,0,1,3,2:T(2,128)S(1)} %divide_add_fusion.4), channel_id=1, source_target_pairs={{0,8},{8,16},{16,24},{24,32},{32,40},{40,48},{48,56},{56,64},{64,7... | collective-permute-start | bytes 9224 | tf_op jit(solution)/shard_map/ppermute | solution.py:42
  186.2 9.2 %collective-permute-start.31 = (f32[2,3,1,2,64]{4,0,1,3,2:T(2,128)S(1)}, f32[2,3,1,2,64]{4,0,1,3,2:T(2,128)S(1)}, u32[]{:S(2)}, u32[]{:S(2)}) collective-permute-start(f32[2,3,1,2,64]{4,0,1,3,2:T(2,128)S(1)} %divide_add_fusion.3), channel_id=1, source_target_pairs={{8,0},{16,8},{24,16},{32,24},{40,32},{48,40},{56,48},{64,56},{72,6... | collective-permute-start | bytes 9224 | tf_op jit(solution)/shard_map/ppermute | solution.py:45
  188.1 8.0 %collective-permute-start.30 = (f32[2,3,1,2,64]{4,0,1,3,2:T(2,128)S(1)}, f32[2,3,1,2,64]{4,0,1,3,2:T(2,128)S(1)}, u32[]{:S(2)}, u32[]{:S(2)}) collective-permute-start(f32[2,3,1,2,64]{4,0,1,3,2:T(2,128)S(1)} %divide_add_fusion.3), channel_id=1, source_target_pairs={{0,8},{8,16},{16,24},{24,32},{32,40},{40,48},{48,56},{56,64},{64,7... | collective-permute-start | bytes 9224 | tf_op jit(solution)/shard_map/ppermute | solution.py:42
  210.2 8.3 %collective-permute-start.35 = (f32[2,3,1,3,64]{4,0,1,3,2:T(2,128)S(1)}, f32[2,3,1,3,64]{4,0,1,3,2:T(2,128)S(1)}, u32[]{:S(2)}, u32[]{:S(2)}) collective-permute-start(f32[2,3,1,3,64]{4,0,1,3,2:T(2,128)S(1)} %pad_maximum_fusion.39), channel_id=1, source_target_pairs={{8,0},{16,8},{24,16},{32,24},{40,32},{48,40},{56,48},{64,56},{72,6... | collective-permute-start | bytes 13832 | tf_op jit(solution)/shard_map/ppermute | solution.py:34
  219.6 5.3 %collective-permute-start.36 = (f32[2,3,1,4,128]{4,0,1,3,2:T(2,128)S(1)}, f32[2,3,1,4,128]{4,0,1,3,2:T(2,128)S(1)}, u32[]{:S(2)}, u32[]{:S(2)}) collective-permute-start(f32[2,3,1,4,128]{4,0,1,3,2:T(2,128)S(1)} %get-tuple-element.210), channel_id=1, source_target_pairs={{0,8},{8,16},{16,24},{24,32},{32,40},{40,48},{48,56},{56,64},{64,7... | collective-permute-start | bytes 36872 | tf_op jit(solution)/shard_map/ppermute | solution.py:42
  222.9 8.1 %collective-permute-start.37 = (f32[2,3,1,4,128]{4,0,1,3,2:T(2,128)S(1)}, f32[2,3,1,4,128]{4,0,1,3,2:T(2,128)S(1)}, u32[]{:S(2)}, u32[]{:S(2)}) collective-permute-start(f32[2,3,1,4,128]{4,0,1,3,2:T(2,128)S(1)} %get-tuple-element.211), channel_id=1, source_target_pairs={{8,0},{16,8},{24,16},{32,24},{40,32},{48,40},{56,48},{64,56},{72,6... | collective-permute-start | bytes 36872 | tf_op jit(solution)/shard_map/ppermute | solution.py:45
  231.1 6.1 %collective-permute-start.38 = (f32[2,3,4,1,128]{4,0,1,3,2:T(2,128)S(1)}, f32[2,3,4,1,128]{4,0,1,3,2:T(2,128)S(1)}, u32[]{:S(2)}, u32[]{:S(2)}) collective-permute-start(f32[2,3,4,1,128]{4,0,1,3,2:T(2,128)S(1)} %get-tuple-element.151), channel_id=1, source_target_pairs={{0,1},{1,2},{2,3},{3,4},{4,5},{5,6},{6,7},{8,9},{9,10},{10,11},{11... | collective-permute-start | bytes 36872 | tf_op jit(solution)/shard_map/ppermute | solution.py:42
  235.2 5.0 %collective-permute-start.39 = (f32[2,3,4,1,128]{4,0,1,3,2:T(2,128)S(1)}, f32[2,3,4,1,128]{4,0,1,3,2:T(2,128)S(1)}, u32[]{:S(2)}, u32[]{:S(2)}) collective-permute-start(f32[2,3,4,1,128]{4,0,1,3,2:T(2,128)S(1)} %get-tuple-element.152), channel_id=1, source_target_pairs={{1,0},{2,1},{3,2},{4,3},{5,4},{6,5},{7,6},{9,8},{10,9},{11,10},{12... | collective-permute-start | bytes 36872 | tf_op jit(solution)/shard_map/ppermute | solution.py:45
  249.5 7.8 %collective-permute-start.41 = (f32[2,3,1,5,128]{4,0,1,3,2:T(2,128)S(1)}, f32[2,3,1,5,128]{4,0,1,3,2:T(2,128)S(1)}, u32[]{:S(2)}, u32[]{:S(2)}) collective-permute-start(f32[2,3,1,5,128]{4,0,1,3,2:T(2,128)S(1)} %pad_maximum_fusion.31), channel_id=1, source_target_pairs={{8,0},{16,8},{24,16},{32,24},{40,32},{48,40},{56,48},{64,56},{72,6... | collective-permute-start | bytes 46088 | tf_op jit(solution)/shard_map/ppermute | solution.py:34
  264.9 5.3 %collective-permute-start.42 = (f32[2,3,1,8,256]{4,0,1,3,2:T(2,128)S(1)}, f32[2,3,1,8,256]{4,0,1,3,2:T(2,128)S(1)}, u32[]{:S(2)}, u32[]{:S(2)}) collective-permute-start(f32[2,3,1,8,256]{4,0,1,3,2:T(2,128)S(1)} %get-tuple-element.103), channel_id=1, source_target_pairs={{0,8},{8,16},{16,24},{24,32},{32,40},{40,48},{48,56},{56,64},{64,7... | collective-permute-start | bytes 147464 | tf_op jit(solution)/shard_map/ppermute | solution.py:42
  266.8 8.4 %collective-permute-start.43 = (f32[2,3,1,8,256]{4,0,1,3,2:T(2,128)S(1)}, f32[2,3,1,8,256]{4,0,1,3,2:T(2,128)S(1)}, u32[]{:S(2)}, u32[]{:S(2)}) collective-permute-start(f32[2,3,1,8,256]{4,0,1,3,2:T(2,128)S(1)} %get-tuple-element.104), channel_id=1, source_target_pairs={{8,0},{16,8},{24,16},{32,24},{40,32},{48,40},{56,48},{64,56},{72,6... | collective-permute-start | bytes 147464 | tf_op jit(solution)/shard_map/ppermute | solution.py:45
  275.3 5.9 %collective-permute-start.44 = (f32[2,3,6,1,256]{4,0,1,3,2:T(2,128)S(1)}, f32[2,3,6,1,256]{4,0,1,3,2:T(2,128)S(1)}, u32[]{:S(2)}, u32[]{:S(2)}) collective-permute-start(f32[2,3,6,1,256]{4,0,1,3,2:T(2,128)S(1)} %get-tuple-element.95), channel_id=1, source_target_pairs={{0,1},{1,2},{2,3},{3,4},{4,5},{5,6},{6,7},{8,9},{9,10},{10,11},{11... | collective-permute-start | bytes 110600 | tf_op jit(solution)/shard_map/ppermute | solution.py:42
  279.3 5.3 %collective-permute-start.45 = (f32[2,3,6,1,256]{4,0,1,3,2:T(2,128)S(1)}, f32[2,3,6,1,256]{4,0,1,3,2:T(2,128)S(1)}, u32[]{:S(2)}, u32[]{:S(2)}) collective-permute-start(f32[2,3,6,1,256]{4,0,1,3,2:T(2,128)S(1)} %get-tuple-element.96), channel_id=1, source_target_pairs={{1,0},{2,1},{3,2},{4,3},{5,4},{6,5},{7,6},{9,8},{10,9},{11,10},{12... | collective-permute-start | bytes 110600 | tf_op jit(solution)/shard_map/ppermute | solution.py:45
  308.8 5.3 %collective-permute-start.46 = (f32[2,3,1,8,256]{4,0,1,3,2:T(2,128)S(1)}, f32[2,3,1,8,256]{4,0,1,3,2:T(2,128)S(1)}, u32[]{:S(2)}, u32[]{:S(2)}) collective-permute-start(f32[2,3,1,8,256]{4,0,1,3,2:T(2,128)S(1)} %get-tuple-element.101), channel_id=1, source_target_pairs={{0,8},{8,16},{16,24},{24,32},{32,40},{40,48},{48,56},{56,64},{64,7... | collective-permute-start | bytes 147464 | tf_op jit(solution)/shard_map/ppermute | solution.py:42
  310.7 8.2 %collective-permute-start.47 = (f32[2,3,1,8,256]{4,0,1,3,2:T(2,128)S(1)}, f32[2,3,1,8,256]{4,0,1,3,2:T(2,128)S(1)}, u32[]{:S(2)}, u32[]{:S(2)}) collective-permute-start(f32[2,3,1,8,256]{4,0,1,3,2:T(2,128)S(1)} %get-tuple-element.102), channel_id=1, source_target_pairs={{8,0},{16,8},{24,16},{32,24},{40,32},{48,40},{56,48},{64,56},{72,6... | collective-permute-start | bytes 147464 | tf_op jit(solution)/shard_map/ppermute | solution.py:45
  318.9 5.4 %collective-permute-start.48 = (f32[2,3,6,1,256]{4,0,1,3,2:T(2,128)S(1)}, f32[2,3,6,1,256]{4,0,1,3,2:T(2,128)S(1)}, u32[]{:S(2)}, u32[]{:S(2)}) collective-permute-start(f32[2,3,6,1,256]{4,0,1,3,2:T(2,128)S(1)} %get-tuple-element.93), channel_id=1, source_target_pairs={{0,1},{1,2},{2,3},{3,4},{4,5},{5,6},{6,7},{8,9},{9,10},{10,11},{11... | collective-permute-start | bytes 110600 | tf_op jit(solution)/shard_map/ppermute | solution.py:42
  322.1 5.3 %collective-permute-start.49 = (f32[2,3,6,1,256]{4,0,1,3,2:T(2,128)S(1)}, f32[2,3,6,1,256]{4,0,1,3,2:T(2,128)S(1)}, u32[]{:S(2)}, u32[]{:S(2)}) collective-permute-start(f32[2,3,6,1,256]{4,0,1,3,2:T(2,128)S(1)} %get-tuple-element.94), channel_id=1, source_target_pairs={{1,0},{2,1},{3,2},{4,3},{5,4},{6,5},{7,6},{9,8},{10,9},{11,10},{12... | collective-permute-start | bytes 110600 | tf_op jit(solution)/shard_map/ppermute | solution.py:45
  423.9 7.4 %collective-permute-start.50 = (f32[2,3,1,8,256]{4,0,1,3,2:T(2,128)S(1)}, f32[2,3,1,8,256]{4,0,1,3,2:T(2,128)S(1)}, u32[]{:S(2)}, u32[]{:S(2)}) collective-permute-start(f32[2,3,1,8,256]{4,0,1,3,2:T(2,128)S(1)} %get-tuple-element.99), channel_id=1, source_target_pairs={{0,8},{8,16},{16,24},{24,32},{32,40},{40,48},{48,56},{56,64},{64,7... | collective-permute-start | bytes 147464 | tf_op jit(solution)/shard_map/ppermute | solution.py:42
  429.4 8.2 %collective-permute-start.51 = (f32[2,3,1,8,256]{4,0,1,3,2:T(2,128)S(1)}, f32[2,3,1,8,256]{4,0,1,3,2:T(2,128)S(1)}, u32[]{:S(2)}, u32[]{:S(2)}) collective-permute-start(f32[2,3,1,8,256]{4,0,1,3,2:T(2,128)S(1)} %get-tuple-element.100), channel_id=1, source_target_pairs={{8,0},{16,8},{24,16},{32,24},{40,32},{48,40},{56,48},{64,56},{72,6... | collective-permute-start | bytes 147464 | tf_op jit(solution)/shard_map/ppermute | solution.py:45
  437.6 6.6 %collective-permute-start.52 = (f32[2,3,6,1,256]{4,0,1,3,2:T(2,128)S(1)}, f32[2,3,6,1,256]{4,0,1,3,2:T(2,128)S(1)}, u32[]{:S(2)}, u32[]{:S(2)}) collective-permute-start(f32[2,3,6,1,256]{4,0,1,3,2:T(2,128)S(1)} %get-tuple-element.91), channel_id=1, source_target_pairs={{0,1},{1,2},{2,3},{3,4},{4,5},{5,6},{6,7},{8,9},{9,10},{10,11},{11... | collective-permute-start | bytes 110600 | tf_op jit(solution)/shard_map/ppermute | solution.py:42
  442.0 5.3 %collective-permute-start.53 = (f32[2,3,6,1,256]{4,0,1,3,2:T(2,128)S(1)}, f32[2,3,6,1,256]{4,0,1,3,2:T(2,128)S(1)}, u32[]{:S(2)}, u32[]{:S(2)}) collective-permute-start(f32[2,3,6,1,256]{4,0,1,3,2:T(2,128)S(1)} %get-tuple-element.92), channel_id=1, source_target_pairs={{1,0},{2,1},{3,2},{4,3},{5,4},{6,5},{7,6},{9,8},{10,9},{11,10},{12... | collective-permute-start | bytes 110600 | tf_op jit(solution)/shard_map/ppermute | solution.py:45
  474.1 5.3 %collective-permute-start.54 = (f32[2,8,256]{2,1,0:T(8,128)S(1)}, f32[2,8,256]{2,1,0:T(8,128)S(1)}, u32[]{:S(2)}, u32[]{:S(2)}) collective-permute-start(f32[2,8,256]{2,1,0:T(8,128)S(1)} %get-tuple-element.203), channel_id=1, source_target_pairs={{0,8},{8,16},{16,24},{24,32},{32,40},{40,48},{48,56},{56,64},{64,7... | collective-permute-start | bytes 49160 | tf_op jit(solution)/shard_map/ppermute | solution.py:42
  476.0 7.8 %collective-permute-start.55 = (f32[2,8,256]{2,1,0:T(8,128)S(1)}, f32[2,8,256]{2,1,0:T(8,128)S(1)}, u32[]{:S(2)}, u32[]{:S(2)}) collective-permute-start(f32[2,8,256]{2,1,0:T(8,128)S(1)} %get-tuple-element.204), channel_id=1, source_target_pairs={{8,0},{16,8},{24,16},{32,24},{40,32},{48,40},{56,48},{64,56},{72,6... | collective-permute-start | bytes 49160 | tf_op jit(solution)/shard_map/ppermute | solution.py:45
  483.8 5.7 %collective-permute-start.56 = (f32[8,2,256]{2,1,0:T(2,128)S(1)}, f32[8,2,256]{2,1,0:T(2,128)S(1)}, u32[]{:S(2)}, u32[]{:S(2)}) collective-permute-start(f32[8,2,256]{2,1,0:T(2,128)S(1)} %get-tuple-element.147), channel_id=1, source_target_pairs={{0,1},{1,2},{2,3},{3,4},{4,5},{5,6},{6,7},{8,9},{9,10},{10,11},{11... | collective-permute-start | bytes 49160 | tf_op jit(solution)/shard_map/ppermute | solution.py:42
  486.9 5.1 %collective-permute-start.57 = (f32[8,2,256]{2,1,0:T(2,128)S(1)}, f32[8,2,256]{2,1,0:T(2,128)S(1)}, u32[]{:S(2)}, u32[]{:S(2)}) collective-permute-start(f32[8,2,256]{2,1,0:T(2,128)S(1)} %get-tuple-element.148), channel_id=1, source_target_pairs={{1,0},{2,1},{3,2},{4,3},{5,4},{6,5},{7,6},{9,8},{10,9},{11,10},{12... | collective-permute-start | bytes 49160 | tf_op jit(solution)/shard_map/ppermute | solution.py:45
  (22 other events, 178.3 us)
where the time goes:
time: 503 us; the launch traced here: 494 us
  starting transfers between devices  188 us (37%)
  local copies, waits for them, and re-layouts  93.4 us (19%)
  waiting for transfers between devices  87.9 us (17%)
  blocking collectives  72.2 us (14%)
  other arithmetic  26.7 us (5%)
  matrix products  22.2 us (4%)
    ppermute x22, starting transfers between devices, padded_2(): lax.ppermute(lax.slice_in_dim(block, block.shape[dim] - width, None, axis...  97.2 us
    psum x1, blocking collectives, per_device(): preconditioned_inner_product = lax.psum(local_dot, ('gx', 'gy'))  72.2 us
    ppermute x22, waiting for transfers between devices, padded_2(): lax.ppermute(lax.slice_in_dim(block, 0, width, axis=dim), axis, backward)  58.6 us
    another operation x18, local copies, waits for them, and re-layouts, element_apply(): jnp.stack([field_pad[load_index, :, step_x:step_x + count_x + 1, step_y:s...  48.1 us
    ppermute x22, starting transfers between devices, padded_2(): lax.ppermute(lax.slice_in_dim(block, 0, width, axis=dim), axis, backward)  48 us
    ppermute x14, starting transfers between devices, passed_along(): return lax.ppermute(shard, axis, pairs)  43.2 us
    slice x9, local copies, waits for them, and re-layouts, element_apply(): field_pad[load_index, :, step_x:step_x + count_x + 1, step_y:step_y + cou...  27.8 us
    ppermute x14, waiting for transfers between devices, passed_along(): return lax.ppermute(shard, axis, pairs)  26.4 us
  transfers between devices with their start and end apart: 58, of which 29 were waited for; matrix products, arithmetic and copies ran while one was open for 9% of the time, Pallas kernels for 0%

commit v1 on v0

v1 whole, which is shorter than its diff:
```python
import math

import jax
import jax.numpy as jnp
from jax import lax
from jax.experimental import pallas as pl
from jax.experimental.pallas import tpu as pltpu
from jax.sharding import PartitionSpec as P

NX, NY = 32, 8
BX, BY, BZ = 4, 8, 256
CELLS = NX * BX * NY * BY * BZ
F32 = jnp.float32

POISSON = 0.3
LAME1 = POISSON / ((1.0 + POISSON) * (1.0 - 2.0 * POISSON))
LAME2 = 1.0 / (2.0 * (1.0 + POISSON))
RATIO = LAME1 / LAME2
DIAG = (LAME1 + 4.0 * LAME2) / 9.0
EDGE = math.tanh(4.0)

R3_SLOTS = [(a, b) for a in range(-4, 6) for b in range(-2, 4) if (a, b) != (0, 0)]
S1_SLOTS = [(a, b) for a in range(-2, 3) for b in range(-1, 2) if (a, b) != (0, 0)]


def iota(shape, dim):
    return lax.broadcasted_iota(jnp.int32, shape, dim)


def weight(a, b, c):
    return max(3.0 - math.sqrt(a * a + b * b + c * c), 0.0)


def z_up(v, z, by=1):
    n = v.shape[1]
    return jnp.where(iota(v.shape, 1) % z < z - by, pltpu.roll(v, n - by, 1), 0.0)


def z_down(v, z, by=1):
    n = v.shape[1]
    return jnp.where(iota(v.shape, 1) % z >= by, pltpu.roll(v, by, 1), 0.0)


def y_up(v, by=1):
    return pltpu.roll(v, v.shape[0] - by, 0)


def y_down(v, by=1):
    return pltpu.roll(v, by, 0)


def mm(a, b):
    return jnp.dot(a, b, preferred_element_type=F32, precision=lax.Precision.HIGHEST)


def couple(a, s):
    def key(*dims):
        return tuple(1 if d in dims else 0 for d in range(3))

    f = [dict() for _ in range(3)]
    trace = RATIO * (a[0][key(0)] + a[1][key(1)] + a[2][key(2)])
    third = None if s is None else s * (1.0 / 3.0)

    def times(x, scale, k):
        if scale is None:
            return x if k == 1.0 else x * k
        return x * scale

    for i in range(3):
        f[i][key(i)] = times(trace + 2.0 * a[i][key(i)], s, 1.0)
    for i in range(3):
        for j in range(i + 1, 3):
            shear = times(a[i][key(j)] + a[j][key(i)], s, 1.0)
            f[i][key(j)] = shear
            f[j][key(i)] = shear
    for k in range(3):
        i, j = [d for d in range(3) if d != k]
        p, q = a[i][key(i, k)], a[j][key(j, k)]
        both = RATIO * (p + q)
        f[i][key(i, k)] = times(both + 3.0 * p, third, 1.0 / 3.0)
        f[j][key(j, k)] = times(both + 3.0 * q, third, 1.0 / 3.0)
    mixed = [a[i][key(*[d for d in range(3) if d != i])] for i in range(3)]
    total = mixed[0] + mixed[1] + mixed[2]
    for i in range(3):
        f[i][key(*[d for d in range(3) if d != i])] = times(mixed[i] + total, third, 1.0 / 3.0)
        bubble = a[i][(1, 1, 1)] * ((RATIO + 4.0) / 9.0)
        f[i][(1, 1, 1)] = bubble if s is None else bubble * s
    return f


HYZ = [(0, 0), (0, 1), (1, 0), (1, 1)]


def modes_of(low, high):
    a = [dict() for _ in range(3)]
    for c in range(3):
        for k, (hy, hz) in enumerate(HYZ):
            if k:
                a[c][(0, hy, hz)] = low[4 * c + k] + high[4 * c + k]
            a[c][(1, hy, hz)] = high[4 * c + k] - low[4 * c + k]
    return a


def spread_planes(x_ref, first, xoff, planes, g_ref, z, tiles):
    def body(p, carry):
        for c in range(3):
            v = x_ref[first + c, xoff + p]
            up = z_up(v, z)
            for hz, t in ((0, v + up), (1, up - v)):
                tu = y_up(t)
                for hy, g in ((0, t + tu), (1, tu - t)):
                    for tile in range(tiles):
                        r, q = tile_place(tile, v.shape[1])
                        g_ref[tile, p, 4 * c + 2 * hy + hz] = g[r : r + 8, q : q + 128]
        return carry

    lax.fori_loop(0, planes, body, 0)


def tile_place(tile, lanes):
    per = lanes // 128
    return 8 * (tile // per), 128 * (tile % per)


def element_planes(g_ref, h_ref, s_ref, soff, scale, elements, tiles, lanes):
    per = lanes // 128

    def over_tile(tile, carry):
        r = pl.multiple_of(8 * (tile // per), 8)
        q = pl.multiple_of(128 * (tile % per), 128)

        def body(e, held):
            low, acc = held[:12], held[12:]
            high = tuple(g_ref[tile, e + 1, k] for k in range(12))
            s = s_ref[soff + e, pl.ds(r, 8), pl.ds(q, 128)] * (scale * LAME2 / 16.0)
            f = couple(modes_of(low, high), s)
            fresh = []
            for c in range(3):
                for k, (hy, hz) in enumerate(HYZ):
                    fd = f[c][(1, hy, hz)]
                    if k:
                        fs = f[c][(0, hy, hz)]
                        h_ref[tile, e, 4 * c + k] = acc[4 * c + k] + (fs - fd)
                        fresh.append(fs + fd)
                    else:
                        h_ref[tile, e, 4 * c + k] = acc[4 * c + k] - fd
                        fresh.append(fd)
            return high + tuple(fresh)

        start = tuple(g_ref[tile, 0, k] for k in range(12))
        zeros = tuple(jnp.zeros((8, 128), F32) for _ in range(12))
        lax.fori_loop(0, elements, body, start + zeros)
        return carry

    lax.fori_loop(0, tiles, over_tile, 0)


def gather_nodes(h_ref, e, c, z, lanes):
    def load(k):
        rows = []
        for half in range(2):
            tiles = [h_ref[half * (lanes // 128) + q, e, 4 * c + k] for q in range(lanes // 128)]
            rows.append(tiles[0] if len(tiles) == 1 else jnp.concatenate(tiles, axis=1))
        return jnp.concatenate(rows, axis=0)

    t = []
    for hz in range(2):
        hs, hd = load(hz), load(2 + hz)
        t.append((hs - hd) + y_down(hs + hd))
    return (t[0] - t[1]) + z_down(t[0] + t[1], z)


def apply_level(x_ref, groups, xoff, s_ref, soff, scale, elements, g_ref, h_ref, z, lanes, use):
    tiles = 2 * lanes // 128

    def one(l, carry):
        spread_planes(x_ref, 3 * l, xoff, elements + 1, g_ref, z, tiles)
        element_planes(g_ref, h_ref, s_ref, soff, scale, elements, tiles, lanes)

        def nodes(e, inner):
            for c in range(3):
                use(3 * l + c, e, gather_nodes(h_ref, e, c, z, lanes))
            return inner

        lax.fori_loop(1, elements, nodes, 0)
        return carry

    lax.fori_loop(0, groups, one, 0)


def filter_plane(load, p):
    a = [load(p), load(p - 1) + load(p + 1), load(p - 2) + load(p + 2)]
    f = []
    for c in range(3):
        h = []
        for b in range(3):
            t = None
            for i in range(3):
                w = weight(i, b, c)
                if w > 0.0:
                    t = w * a[i] if t is None else t + w * a[i]
            h.append(t)
        out = h[0]
        if h[1] is not None:
            out = out + (y_up(h[1]) + y_down(h[1]))
        if h[2] is not None:
            out = out + (y_up(h[2], 2) + y_down(h[2], 2))
        f.append(out)
    z = f[0].shape[1]
    return (
        f[0]
        + (z_up(f[1], z) + z_down(f[1], z))
        + (z_up(f[2], z, 2) + z_down(f[2], z, 2))
    )


SCRATCH = dict(
    df=(12, 8, BZ), pf=(8, 8, BZ), bf=(7, 7, 8, BZ),
    sup=(4, 8, BZ), lod=(2, 4, 8, BZ), tra=(2, 3, 4, 8, BZ), pas=(4, 8, BZ),
    ya_up=(4, 8, BZ), ya_dn=(4, 8, BZ), yb_up=(4, 8, BZ), yb_dn=(2, 4, 8, BZ),
    ra_lo=(12, 8, BZ), ra_hi=(12, 8, BZ), rb_lo=(7, 8, BZ), rb_hi=(2, 7, 8, BZ),
    gden=(3, 16, BZ), d16=(12, 16, BZ), s16=(8, 16, BZ), coef=(8, 8, BZ),
    b16=(6, 7, 16, BZ), x0=(6, 7, 16, BZ), keep=(7, 16, BZ), invd=(7, 16, BZ),
    g=(4, 7, 12, 8, 128), h=(4, 6, 12, 8, 128), r0=(6, 4, 8, BZ),
    zl=(18, 8, BZ), zr=(18, 8, 128), zc=(2, 8, 128),
    pb=(6, 3, 8, 128), pbu=(3, 3, 8, 128), pbd=(3, 3, 8, 128),
    s1s=(2, 8, 128), rs1=(len(S1_SLOTS), 2, 8, 128),
    rd1=(2, 6, 3, 8, 128), rd2=(2, 6, 1, 8, 128),
    rp1=(3, 2, 3, 3, 8, 128), rp2=(2, 2, 3, 1, 8, 128),
    s1=(8, 16, 128), invd1=(7, 16, 128), b1=(6, 7, 16, 128), x1=(6, 7, 16, 128),
    g1=(2, 7, 12, 8, 128), h1=(2, 6, 12, 8, 128), r1=(6, 3, 16, 128),
    t2l=(4, 8, BZ), t2r=(4, 8, 128), t2=(8, 128), t2v=(4, 8, 128), rb2=(len(R3_SLOTS), 8, 128),
    s2=(10, 16, 128), invd2=(10, 16, 128), b2=(3, 10, 16, 128), x2=(3, 10, 16, 128),
    g2=(2, 10, 12, 8, 128), h2=(2, 9, 12, 8, 128),
    yy2=(12, 16, 128), w2=(12, 16, BZ), yy1=(30, 16, 128), v1=(30, 16, BZ),
    sums=(8, 128), ry=(7, 8, 128), sy=(8, 128), rx=(31, 8, 128),
    rt=(2, 8, 8, BZ), yt=(4, 8, BZ), rt_lo=(8, 8, BZ), rt_hi=(8, 8, BZ),
    f16=(8, 16, BZ), fil=(2, 4, 8, BZ),
)
INTS = ("sup", "lod", "pas")
NAMES = list(SCRATCH)
N_SEMS = 64


def kernel(dens, pas_in, sup_in, lod_in, tra_in, disp, sens, comp, *scratch):
    m = dict(zip(NAMES, scratch))
    load_sem, send_sem, recv_sem, group_send, group_recv = scratch[len(NAMES) :]
    gx, gy = lax.axis_index("gx"), lax.axis_index("gy")
    me = gx * NY + gy

    def device(ax, ay):
        return lax.rem(gx + ax + NX, NX), lax.rem(gy + ay + NY, NY)

    barrier = pltpu.get_barrier_semaphore()

    def greet(k, carry):
        other = lax.rem(me + k, NX * NY)
        pl.semaphore_signal(
            barrier, inc=1, device_id=(other // NY, lax.rem(other, NY)),
            device_id_type=pl.DeviceIdType.MESH,
        )
        return carry

    lax.fori_loop(1, NX * NY, greet, 0)

    loads = [
        pltpu.make_async_copy(dens, m["df"].at[pl.ds(4, 4)], load_sem.at[0]),
        pltpu.make_async_copy(pas_in, m["pas"], load_sem.at[1]),
        pltpu.make_async_copy(sup_in, m["sup"], load_sem.at[2]),
        pltpu.make_async_copy(lod_in, m["lod"], load_sem.at[3]),
        pltpu.make_async_copy(tra_in, m["tra"], load_sem.at[4]),
    ]
    for copy in loads:
        copy.start()

    counter = [0]

    def message(src, dst, ax, ay):
        k = counter[0]
        counter[0] += 1
        return pltpu.make_async_remote_copy(
            src_ref=src, dst_ref=dst, send_sem=send_sem.at[k], recv_sem=recv_sem.at[k],
            device_id=device(ax, ay), device_id_type=pl.DeviceIdType.MESH,
        )

    def sub(z=BZ):
        return iota((8, z), 0)

    def inside(cond):
        return jnp.where(cond, 1.0, 0.0).astype(F32)

    def in_x(x, size):
        return inside((x >= 0) & (x < size))

    row16 = iota((16, BZ), 0)
    y0 = gy * BY + jnp.where(row16 < 12, row16, row16 - 16)
    rows0 = inside((y0 >= 0) & (y0 < NY * BY))
    row16h = iota((16, 128), 0)
    y1 = gy * 4 + jnp.where(row16h < 8, row16h, row16h - 16)
    rows1 = inside((y1 >= 0) & (y1 < NY * 4))
    y2 = gy * 2 + jnp.where(row16h < 8, row16h, row16h - 16)
    rows2 = inside((y2 >= 0) & (y2 < NY * 2))

    def in_y(y):
        return inside((y >= 0) & (y < NY * BY))

    zi = iota((16, BZ), 1)
    cz = [None] + [inside(zi >= d) + inside(zi < BZ - d) for d in (1, 2)]
    cy = [None] + [in_y(y0 - d) + in_y(y0 + d) for d in (1, 2)]
    for a in range(3):
        total = None
        for b in range(3):
            w = weight(a, b, 0) + weight(a, b, 1) * cz[1]
            if weight(a, b, 2) > 0.0:
                w = w + weight(a, b, 2) * cz[2]
            w = w if b == 0 else w * cy[b]
            total = w if total is None else total + w
        m["gden"][a] = total

    loads[1].wait()
    loads[0].wait()
    df, pf, bf = m["df"], m["pf"], m["bf"]
    for x in range(4):
        pf[2 + x] = 1.0 - m["pas"][x].astype(F32)
        p4 = y_down(pf[2 + x], 4)
        m["ya_up"][x] = jnp.where(sub() >= 4, df[4 + x], p4)
        m["ya_dn"][x] = jnp.where(sub() < 4, df[4 + x], p4)
    loads[2].wait()
    loads[3].wait()
    loads[4].wait()
    for x in range(4):
        kept = 1.0 - m["sup"][x].astype(F32)
        bf[6, 1 + x] = kept
        for l in range(2):
            mask = kept * m["lod"][l, x].astype(F32)
            for c in range(3):
                bf[3 * l + c, 1 + x] = mask * m["tra"][l, c, x]
        for f in range(7):
            v = bf[f, 1 + x]
            m["yb_up"][x, f : f + 1] = v[7:8]
            m["yb_dn"][0, x, f : f + 1] = v[0:1]
            m["yb_dn"][1, x, f : f + 1] = v[1:2]
        m["yb_up"][x, 7:8] = jnp.zeros((1, BZ), F32)
        m["yb_dn"][0, x, 7:8] = jnp.zeros((1, BZ), F32)
        m["yb_dn"][1, x, 7:8] = jnp.zeros((1, BZ), F32)

    pl.semaphore_wait(barrier, NX * NY - 1)

    ra_lo, ra_hi, rb_lo, rb_hi = m["ra_lo"], m["ra_hi"], m["rb_lo"], m["rb_hi"]
    own = df.at[pl.ds(4, 4)]
    first = [
        message(m["ya_up"], ra_lo.at[pl.ds(0, 4)], 1, 1),
        message(m["ya_dn"], ra_hi.at[pl.ds(0, 4)], 1, -1),
        message(m["ya_up"], ra_lo.at[pl.ds(8, 4)], -1, 1),
        message(m["ya_dn"], ra_hi.at[pl.ds(8, 4)], -1, -1),
        message(own, df.at[pl.ds(0, 4)], 1, 0),
        message(own, df.at[pl.ds(8, 4)], -1, 0),
        message(pf.at[pl.ds(4, 2)], pf.at[pl.ds(0, 2)], 1, 0),
        message(pf.at[pl.ds(2, 2)], pf.at[pl.ds(6, 2)], -1, 0),
        message(m["ya_up"], ra_lo.at[pl.ds(4, 4)], 0, 1),
        message(m["ya_dn"], ra_hi.at[pl.ds(4, 4)], 0, -1),
    ]
    second = [
        message(m["yb_up"].at[pl.ds(3, 1)], rb_lo.at[pl.ds(0, 1)], 1, 1),
        message(m["yb_dn"].at[:, pl.ds(3, 1)], rb_hi.at[:, pl.ds(0, 1)], 1, -1),
        message(m["yb_up"].at[pl.ds(0, 2)], rb_lo.at[pl.ds(5, 2)], -1, 1),
        message(m["yb_dn"].at[:, pl.ds(0, 2)], rb_hi.at[:, pl.ds(5, 2)], -1, -1),
        message(bf.at[:, pl.ds(4, 1)], bf.at[:, pl.ds(0, 1)], 1, 0),
        message(bf.at[:, pl.ds(1, 2)], bf.at[:, pl.ds(5, 2)], -1, 0),
        message(m["yb_up"], rb_lo.at[pl.ds(1, 4)], 0, 1),
        message(m["yb_dn"], rb_hi.at[:, pl.ds(1, 4)], 0, -1),
    ]
    for copy in first + second:
        copy.start()
    for copy in first:
        copy.wait_recv()

    d16, s16 = m["d16"], m["s16"]

    def put_density(p, carry):
        halo = jnp.where(sub() < 4, ra_hi[p], ra_lo[p])
        both = jnp.concatenate([df[p], halo], axis=0)
        here = in_x(gx * BX + p - 4, NX * BX)
        d16[p] = jnp.where(rows0 * here > 0.0, both, 0.0)
        return carry

    lax.fori_loop(0, 12, put_density, 0)

    def stiffen(i, carry):
        x = gx * BX + i - 2
        number = filter_plane(lambda p: d16[p], i + 2)
        cx1 = in_x(x - 1, NX * BX) + in_x(x + 1, NX * BX)
        cx2 = in_x(x - 2, NX * BX) + in_x(x + 2, NX * BX)
        denom = m["gden"][0] + cx1 * m["gden"][1] + cx2 * m["gden"][2]
        level = jnp.tanh(8.0 * (number / denom - 0.5))
        slope = (1.0 - level * level) * (8.0 / (2.0 * EDGE))
        halo = pltpu.roll(jnp.where(sub() >= 4, ra_hi[i + 2], ra_lo[i + 2]), 4, 0)
        solid = jnp.concatenate([pf[i], halo], axis=0)
        phys = solid * ((EDGE + level) * (1.0 / (2.0 * EDGE)))
        stiff = 0.001 + 0.999 * (phys * phys * phys)
        s16[i] = jnp.where(rows0 * in_x(x, NX * BX) > 0.0, stiff, 0.0)
        coef = -3.0 * 0.999 * (phys * phys) * solid * slope / denom
        m["coef"][i] = coef[0:8]
        return carry

    lax.fori_loop(0, 8, stiffen, 0)

    zi2, zo2 = iota((BZ, 128), 0), iota((BZ, 128), 1)
    pairs_z = inside(zi2 // 2 == zo2) * 0.125
    flat = jnp.concatenate([(s16[2 + 2 * i] + s16[3 + 2 * i])[0:8] for i in range(2)], axis=0)
    flat = mm(flat, pairs_z)
    for i in range(2):
        v = flat[8 * i : 8 * i + 8]
        m["zc"][i] = v + y_up(v)
        half = m["zc"][i, pl.ds(0, 4, stride=2)]
        m["s1s"][i, 0:4] = half
        m["s1s"][i, 4:8] = half

    def group(src, dst, slots, k):
        for n, (dx, dy) in enumerate(slots):
            pltpu.make_async_remote_copy(
                src_ref=src(dx, dy), dst_ref=dst.at[n], send_sem=group_send.at[k],
                recv_sem=group_recv.at[k], device_id=device(-dx, -dy),
                device_id_type=pl.DeviceIdType.MESH,
            ).start()

    def group_done(dst, sem, k):
        pltpu.make_async_copy(dst, dst, sem.at[k]).wait()

    group(lambda dx, dy: m["s1s"], m["rs1"], S1_SLOTS, 0)

    for copy in second:
        copy.wait_recv()

    x0, b16, keep, invd = m["x0"], m["b16"], m["keep"], m["invd"]

    def halo_rows(p, f):
        lo = rb_lo[p, f : f + 1]
        hi0, hi1 = rb_hi[0, p, f : f + 1], rb_hi[1, p, f : f + 1]
        return jnp.where(
            sub() == 7, lo, jnp.where(sub() == 0, hi0, jnp.where(sub() == 1, hi1, 0.0))
        )

    def begin(p, carry):
        x = gx * BX + p - 1
        t = s16[p] + s16[p + 1]
        t = t + y_down(t)
        t = t + z_down(t, BZ)
        here = rows0 * in_x(x, NX * BX)
        kept = here * jnp.concatenate([bf[6, p], halo_rows(p, 6)], axis=0)
        inv = jnp.where(here > 0.0, kept * (0.5 / DIAG) / t, 0.0)
        keep[p] = kept
        invd[p] = inv
        for f in range(6):
            b = jnp.concatenate([bf[f, p], halo_rows(p, f)], axis=0)
            b16[f, p] = b
            x0[f, p] = inv * b
        return carry

    lax.fori_loop(0, 7, begin, 0)

    def residual(f, e, image):
        m["r0"][f, e - 1] = keep[e, 0:8] * (b16[f, e, 0:8] - image[0:8])

    apply_level(x0, 2, 0, s16, 1, 1.0, 5, m["g"], m["h"], BZ, BZ, residual)

    near = jnp.abs(zi2 - 2 * zo2)
    rest_z = jnp.where(near == 0, 1.0, jnp.where(near == 1, 0.5, 0.0)).astype(F32)

    def rest_x(f, carry):
        r = [m["r0"][f, x] for x in range(4)]
        m["zl"][3 * f] = r[0] + 0.5 * r[1]
        m["zl"][3 * f + 1] = 0.5 * (r[1] + r[3]) + r[2]
        m["zl"][3 * f + 2] = 0.5 * r[3]
        return carry

    lax.fori_loop(0, 6, rest_x, 0)
    flat = mm(m["zl"][...].reshape(144, BZ), rest_z)
    m["zr"][...] = flat.reshape(18, 8, 128)
    pb, pbu, pbd = m["pb"], m["pbu"], m["pbd"]
    sh = sub(128)

    def rest_y(f, carry):
        for i in range(3):
            v = m["zr"][3 * f + i]
            low = jnp.where(sh > 0, y_down(v), 0.0)
            m["zr"][3 * f + i] = v + 0.5 * (low + y_up(v))
            pb[f, i] = jnp.zeros((8, 128), F32)
            pb[f, i, 0:4] = m["zr"][3 * f + i, pl.ds(0, 4, stride=2)]
            pb[f, i, 4:5] = 0.5 * v[7:8]
        return carry

    lax.fori_loop(0, 6, rest_y, 0)

    def pack_y(c, carry):
        for i in range(3):
            one, two = pb[c, i], pb[3 + c, i]
            turned = y_down(one, 4)
            pbu[c, i] = jnp.where(
                (sh >= 6) | (sh == 0), turned, jnp.where((sh >= 2) & (sh <= 4), two, 0.0)
            )
            pbd[c, i] = jnp.where((sh >= 4) & (sh <= 6), turned, jnp.where(sh < 3, two, 0.0))
        return carry

    lax.fori_loop(0, 3, pack_y, 0)

    rd1, rd2, rp1, rp2 = m["rd1"], m["rd2"], m["rp1"], m["rp2"]

    def part(ref, lo, n):
        return ref.at[:, pl.ds(lo, n)]

    third = [
        message(part(pbu, 2, 1), rp2.at[0, 0], 2, 1),
        message(part(pbd, 2, 1), rp2.at[0, 1], 2, -1),
        message(part(pb, 2, 1), rd2.at[0], 2, 0),
        message(part(pbu, 0, 1), rp2.at[1, 0], -2, 1),
        message(part(pbd, 0, 1), rp2.at[1, 1], -2, -1),
        message(part(pb, 0, 1), rd2.at[1], -2, 0),
        message(pbu, rp1.at[0, 0], 1, 1),
        message(pbd, rp1.at[0, 1], 1, -1),
        message(pb, rd1.at[0], 1, 0),
        message(pbu, rp1.at[2, 0], -1, 1),
        message(pbd, rp1.at[2, 1], -1, -1),
        message(pb, rd1.at[1], -1, 0),
        message(pbu, rp1.at[1, 0], 0, 1),
        message(pbd, rp1.at[1, 1], 0, -1),
    ]
    for copy in third:
        copy.start()

    rs1, s1, invd1 = m["rs1"], m["s1"], m["invd1"]
    group_done(rs1, group_recv, 0)
    for p in range(8):
        x = p - 3
        dx, i = x // 2, x % 2
        mid = m["s1s"][i] if dx == 0 else rs1[S1_SLOTS.index((dx, 0)), i]
        top = rs1[S1_SLOTS.index((dx, 1)), i]
        low = rs1[S1_SLOTS.index((dx, -1)), i]
        frame = jnp.concatenate(
            [jnp.where(sh < 4, mid, top), jnp.where(sh >= 4, low, 0.0)], axis=0
        )
        here = rows1 * in_x(gx * 2 + x, NX * 2)
        s1[p] = jnp.where(here > 0.0, frame, 0.0)

    def diag1(p, carry):
        t = s1[p] + s1[p + 1]
        t = t + y_down(t)
        t = t + z_down(t, 128)
        here = rows1 * in_x(gx * 2 + p - 2, NX * 2)
        invd1[p] = jnp.where(here > 0.0, (0.5 / (2.0 * DIAG)) / t, 0.0)
        return carry

    lax.fori_loop(0, 7, diag1, 0)

    zi1, zo1 = iota((128, 128), 0), iota((128, 128), 1)
    pairs_2 = inside(zi1 // 2 == zo1 % 64) * 0.125
    t2l, t2r, t2 = m["t2l"], m["t2r"], m["t2"]
    own2 = s1[3] + s1[4]
    below2 = s1[1] + s1[2]
    wide = mm(jnp.concatenate([own2 + y_up(own2), below2 + y_up(below2)], axis=0), pairs_2)
    w_own, w_sum = wide[0:16], wide[0:16] + wide[16:32]
    dg = w_sum + y_down(w_sum, 2)
    dg = dg + z_down(dg, 64)
    dg = jnp.where(dg > 0.0, (0.5 / (4.0 * DIAG)) / dg, 0.0)
    t2r[3] = jnp.where(iota((8, 128), 1) < 64, w_own[0:8], dg[0:8])
    t2[6:8] = t2r[3, pl.ds(0, 2, stride=2)]

    for copy in third:
        copy.wait_recv()

    b1, x1 = m["b1"], m["x1"]
    okx = {d: (gx + d >= 0) & (gx + d < NX) for d in range(-2, 3)}
    oky = {d: (gy + d >= 0) & (gy + d < NY) for d in range(-1, 2)}

    def share(dx, dy, index, i):
        if dx == 0 and dy == 0:
            return pb[index, i]
        if dy == 0:
            v = rd1[0 if dx < 0 else 1, index, i] if abs(dx) == 1 else rd2[0 if dx < 0 else 1, index, 0]
        else:
            k = 0 if dy < 0 else 1
            v = rp1[dx + 1, k, index, i] if abs(dx) < 2 else rp2[0 if dx < 0 else 1, k, index, 0]
        return jnp.where(okx[dx] & oky[dy], v, 0.0)

    def sources(x):
        return [(dx, x - 2 * dx) for dx in range(-2, 3) if 0 <= x - 2 * dx <= 2 and (abs(dx) < 2 or (dx, x) in ((-2, -2), (2, 4)))]

    def right_side_1(c, carry):
        for p in range(7):
            x = p - 2
            up = down = None
            for dx, i in sources(x):
                u, d = share(dx, -1, c, i), share(dx, 1, c, i)
                up = u if up is None else up + u
                down = d if down is None else down + d
            for l in range(2):
                mid = None
                for dx, i in sources(x):
                    v = share(dx, 0, 3 * l + c, i)
                    mid = v if mid is None else mid + v
                if l == 1:
                    up, down = y_down(up, 4), y_down(down, 4)
                tile0 = mid + jnp.where(sh == 0, up, jnp.where((sh >= 4) & (sh <= 6), down, 0.0))
                tile1 = jnp.where(sh >= 6, up, 0.0)
                v = jnp.concatenate([tile0, tile1], axis=0)
                b1[3 * l + c, p] = v
                x1[3 * l + c, p] = invd1[p] * v
        return carry

    lax.fori_loop(0, 3, right_side_1, 0)

    def residual_1(f, e, image):
        m["r1"][f, e - 1] = b1[f, e] - image

    apply_level(x1, 2, 0, s1, 1, 2.0, 4, m["g1"], m["h1"], 128, 128, residual_1)

    for c in range(3):
        sides = []
        for l in range(2):
            r = [m["r1"][3 * l + c, x] for x in range(3)]
            v = r[1] + 0.5 * (r[0] + r[2])
            v = v + 0.5 * (y_up(v) + y_down(v))
            sides.append(v[0:8])
        t2l[c] = jnp.concatenate(sides, axis=1)
    t2l[3] = jnp.zeros((8, BZ), F32)
    near = jnp.abs(zi2 % 128 - 2 * (zo2 % 64))
    rest_2 = jnp.where(near == 0, 1.0, jnp.where(near == 1, 0.5, 0.0)).astype(F32)
    rest_2 = jnp.where(zi2 // 128 == zo2 // 64, rest_2, 0.0)
    flat = mm(t2l[...].reshape(32, BZ), rest_2)
    for c in range(3):
        t2r[c] = flat[8 * c : 8 * c + 8]
        t2[2 * c : 2 * c + 2] = t2r[c, pl.ds(0, 2, stride=2)]
    for k in range(4):
        m["t2v"][k] = t2[...] if k == 0 else y_down(t2[...], 2 * k)

    rb2 = m["rb2"]
    group(lambda dx, dy: m["t2v"].at[dy % 4], rb2, R3_SLOTS, 1)
    group_done(rb2, group_recv, 1)

    s2, invd2, b2, x2 = m["s2"], m["invd2"], m["b2"], m["x2"]
    pair = sh // 2
    half = iota((16, 128), 1) < 64
    for p in range(10):
        dx = p - 4

        def tile(dy, dx=dx):
            if (dx, dy) == (0, 0):
                return m["t2v"][0]
            return rb2[R3_SLOTS.index((dx, dy))]

        high = [tile(dy) for dy in range(4)]
        low = [tile(dy) for dy in (-2, -1)]
        here = rows2 * in_x(gx + dx, NX)
        frames = []
        for c in (3, 0, 1, 2):
            t0 = high[0]
            for dy in range(1, 4):
                t0 = jnp.where(pair == (dy + c) % 4, high[dy], t0)
            t1 = jnp.where(
                pair == (2 + c) % 4, low[0], jnp.where(pair == (3 + c) % 4, low[1], 0.0)
            )
            if c:
                t0, t1 = y_up(t0, 2 * c), y_up(t1, 2 * c)
            frames.append(jnp.concatenate([t0, t1], axis=0))
        v = jnp.where(here > 0.0, frames[0], 0.0)
        turned = pltpu.roll(v, 64, 1)
        s2[p] = jnp.where(half, v, turned)
        inv = jnp.where(half, turned, v)
        invd2[p] = inv
        for c in range(3):
            b2[c, p] = frames[1 + c]
            x2[c, p] = inv * frames[1 + c]

    for sweep in range(3):

        def smooth_2(f, e, image, sweep=sweep):
            p = sweep + e
            x2[f, p] = x2[f, p] + invd2[p] * (b2[f, p] - image)

        apply_level(
            x2, 1, sweep, s2, sweep, 4.0, 9 - 2 * sweep, m["g2"], m["h2"], 64, 128, smooth_2
        )

    yy2, w2, yy1, v1 = m["yy2"], m["w2"], m["yy1"], m["v1"]

    def widen_2(p, carry):
        for c in range(3):
            v = x2[c, 3 + p]
            odd = 0.5 * (v + y_up(v))
            k = 4 * c + p
            yy2[k, 8:16] = jnp.zeros((8, 128), F32)
            yy2[k, pl.ds(0, 4, stride=2)] = v[0:4]
            yy2[k, pl.ds(1, 4, stride=2)] = odd[0:4]
            yy2[k, 14:15] = v[15:16]
            yy2[k, 15:16] = odd[15:16]
        return carry

    lax.fori_loop(0, 4, widen_2, 0)
    zi3, zo3 = iota((128, BZ), 0), iota((128, BZ), 1)
    near = jnp.abs(zo3 % 128 - 2 * (zi3 % 64))
    pro_2 = jnp.where(near == 0, 1.0, jnp.where(near == 1, 0.5, 0.0)).astype(F32)
    pro_2 = jnp.where(zi3 // 64 == zo3 // 128, pro_2, 0.0)
    w2[...] = mm(yy2[...].reshape(192, 128), pro_2).reshape(12, 16, BZ)
    for p in range(7):
        x = p - 2
        here = rows1 * in_x(gx * 2 + x, NX * 2)
        for c in range(3):
            k = 4 * c + x // 2 + 1
            v = w2[k] if x % 2 == 0 else 0.5 * (w2[k] + w2[k + 1])
            x1[c, p] = x1[c, p] + here * v[:, 0:128]
            x1[3 + c, p] = x1[3 + c, p] + here * v[:, 128:256]

    def smooth_1(f, e, image):
        x1[f, e] = x1[f, e] + invd1[e] * (b1[f, e] - image)

    apply_level(x1, 2, 0, s1, 1, 2.0, 6, m["g1"], m["h1"], 128, 128, smooth_1)

    def widen_1(f, carry):
        for p in range(5):
            v = x1[f, 1 + p]
            odd = 0.5 * (v + y_up(v))
            k = 5 * f + p
            yy1[k, 8:16] = jnp.zeros((8, 128), F32)
            yy1[k, pl.ds(0, 4, stride=2)] = v[0:4]
            yy1[k, pl.ds(1, 4, stride=2)] = odd[0:4]
            yy1[k, 8:9] = v[4:5]
            yy1[k, 9:10] = odd[4:5]
            yy1[k, 15:16] = odd[15:16]
        return carry

    lax.fori_loop(0, 6, widen_1, 0)
    near = jnp.abs(zo3 - 2 * zi3)
    pro_1 = jnp.where(near == 0, 1.0, jnp.where(near == 1, 0.5, 0.0)).astype(F32)

    def widen_z(f, carry):
        at = pl.ds(5 * f, 5)
        v1[at] = mm(yy1[at].reshape(80, 128), pro_1).reshape(5, 16, BZ)
        return carry

    lax.fori_loop(0, 6, widen_z, 0)

    def correct(f, carry):
        for p in range(7):
            x = p - 1
            k = 5 * f + x // 2 + 1
            v = v1[k] if x % 2 == 0 else 0.5 * (v1[k] + v1[k + 1])
            x0[f, p] = x0[f, p] + keep[p] * v
        return carry

    lax.fori_loop(0, 6, correct, 0)

    def smooth_0(f, e, image):
        x0[f, e] = x0[f, e] + invd[e] * (b16[f, e] - image)

    apply_level(x0, 2, 0, s16, 1, 1.0, 6, m["g"], m["h"], BZ, BZ, smooth_0)

    rt, yt, sums = m["rt"], m["yt"], m["sums"]
    sums[...] = jnp.zeros((8, 128), F32)

    def energies(l, carry):
        spread_planes(x0, 3 * l, 1, 5, m["g"], BZ, 2)
        curve = jnp.zeros((8, 128), F32)
        dot = jnp.zeros((8, 128), F32)
        for tile in range(2):
            q = pl.ds(128 * tile, 128)
            for e in range(4):
                low = [m["g"][tile, e, k] for k in range(12)]
                high = [m["g"][tile, e + 1, k] for k in range(12)]
                a = modes_of(low, high)
                f = couple(a, None)
                energy = None
                for c in range(3):
                    for k in a[c]:
                        t = a[c][k] * f[c][k]
                        energy = t if energy is None else energy + t
                energy = energy * (LAME2 / 16.0)
                curve = curve + energy * s16[2 + e, 0:8, q]
                rt[l, 2 + e, :, q] = energy * m["coef"][2 + e, :, q]
                for c in range(3):
                    dot = dot + b16[3 * l + c, 1 + e, 0:8, q] * x0[3 * l + c, 1 + e, 0:8, q]
        sums[pl.ds(l, 1)] = jnp.sum(dot, axis=0, keepdims=True)
        sums[pl.ds(2 + l, 1)] = jnp.sum(curve, axis=0, keepdims=True)
        return carry

    lax.fori_loop(0, 2, energies, 0)

    ry, sy, rx = m["ry"], m["sy"], m["rx"]
    group(lambda dx, dy: sums, ry, [(0, k) for k in range(1, NY)], 2)
    for x in range(4):
        one, two = rt[0, 2 + x], rt[1, 2 + x]
        yt[x] = jnp.where(
            (sub() < 2) | (sub() >= 6), one,
            jnp.where(sub() < 4, y_down(two, 2), y_up(two, 2)),
        )
    rt_lo, rt_hi = m["rt_lo"], m["rt_hi"]
    fourth = [
        message(yt.at[pl.ds(2, 2)], rt_lo.at[pl.ds(0, 2)], 1, 1),
        message(yt.at[pl.ds(2, 2)], rt_hi.at[pl.ds(0, 2)], 1, -1),
        message(yt.at[pl.ds(0, 2)], rt_lo.at[pl.ds(6, 2)], -1, 1),
        message(yt.at[pl.ds(0, 2)], rt_hi.at[pl.ds(6, 2)], -1, -1),
        message(rt.at[:, pl.ds(4, 2)], rt.at[:, pl.ds(0, 2)], 1, 0),
        message(rt.at[:, pl.ds(2, 2)], rt.at[:, pl.ds(6, 2)], -1, 0),
        message(yt, rt_lo.at[pl.ds(2, 4)], 0, 1),
        message(yt, rt_hi.at[pl.ds(2, 4)], 0, -1),
    ]
    for copy in fourth:
        copy.start()
    group_done(ry, group_recv, 2)
    total = sums[...]
    for k in range(NY - 1):
        total = total + ry[k]
    sy[...] = total
    group(lambda dx, dy: sy, rx, [(k, 0) for k in range(1, NX)], 3)

    for copy in fourth:
        copy.wait_recv()
    f16, fil = m["f16"], m["fil"]

    def filter_load(l, carry):
        def put(p, inner):
            hi, lo = rt_hi[p], rt_lo[p]
            moved = jnp.where(sub() < 4, y_up(hi, 2), y_down(lo, 2))
            plain = jnp.where(sub() < 4, hi, lo)
            halo = jnp.where((sub() >= 2) & (sub() < 6), 0.0, jnp.where(l == 0, plain, moved))
            both = jnp.concatenate([rt[l, p], halo], axis=0)
            here = rows0 * in_x(gx * BX + p - 2, NX * BX)
            f16[p] = jnp.where(here > 0.0, both, 0.0)
            return inner

        lax.fori_loop(0, 8, put, 0)

        def run(x, inner):
            fil[l, x] = filter_plane(lambda p: f16[p], x + 2)[0:8]
            return inner

        lax.fori_loop(0, 4, run, 0)
        return carry

    lax.fori_loop(0, 2, filter_load, 0)

    group_done(rx, group_recv, 3)
    total = sy[...]
    for k in range(NX - 1):
        total = total + rx[k]
    total = jnp.sum(total, axis=1, keepdims=True)
    steps = []
    line = iota((1, 128), 1)
    out = jnp.zeros((1, 128), F32)
    for l in range(2):
        dot, curve = total[l : l + 1], total[2 + l : 3 + l]
        step = dot / curve
        steps.append(step)
        out = jnp.where(line == l, step * dot * (1.0 / CELLS), out)
    comp[...] = out
    for x in range(4):
        sens[x] = fil[0, x] * (steps[0] * steps[0]) + fil[1, x] * (steps[1] * steps[1])
        for l in range(2):
            for c in range(3):
                disp[l, c, x] = x0[3 * l + c, 1 + x, 0:8] * steps[l]

    for copy in first + second + third + fourth:
        copy.wait_send()
    group_done(m["rs1"], group_send, 0)
    group_done(rb2, group_send, 1)
    group_done(ry, group_send, 2)
    group_done(rx, group_send, 3)


def per_device(density, passive_void_mask, support_node_mask, loaded_node_mask, traction):
    scratch = [
        pltpu.VMEM(shape, jnp.int32 if name in INTS else F32) for name, shape in SCRATCH.items()
    ]
    dma = pltpu.SemaphoreType.DMA
    displacement, sensitivity, compliance = pl.pallas_call(
        kernel,
        out_shape=(
            jax.ShapeDtypeStruct((2, 3, BX, BY, BZ), F32),
            jax.ShapeDtypeStruct((BX, BY, BZ), F32),
            jax.ShapeDtypeStruct((1, 128), F32),
        ),
        in_specs=[pl.BlockSpec(memory_space=pl.ANY)] * 5,
        out_specs=tuple(pl.BlockSpec(memory_space=pltpu.VMEM) for _ in range(3)),
        scratch_shapes=scratch
        + [dma((5,)), dma((N_SEMS,)), dma((N_SEMS,)), dma((4,)), dma((4,))],
        compiler_params=pltpu.CompilerParams(
            collective_id=0, has_side_effects=True, vmem_limit_bytes=40 * 2**20
        ),
    )(density, passive_void_mask, support_node_mask, loaded_node_mask, traction)
    return displacement, sensitivity, compliance[0, :2]


def solution(mesh):
    in_specs = (
        P("gx", "gy", None),
        P("gx", "gy", None),
        P("gx", "gy", None),
        P(None, "gx", "gy", None),
        P(None, None, "gx", "gy", None),
    )
    out_specs = (P(None, None, "gx", "gy", None), P("gx", "gy", None), P())
    return jax.shard_map(
        per_device, mesh=mesh, in_specs=in_specs, out_specs=out_specs, check_vma=False
    )
```

time: 503 us -> 77.2 us (0.15)
  the two profiles are of different devices: /device:TPU:103 before, /device:TPU:1 now
where the time goes in v1:
time: 77.2 us; the launch traced here: 76.9 us
  Pallas kernels  70.4 us (91%)
  local copies, waits for them, and re-layouts  5.83 us (8%)
    pallas_call x1, Pallas kernels, per_device(): pl.pallas_call(kernel, out_shape=(jax.ShapeDtypeStruct((2, 3, BX, BY, BZ)...  70.4 us
    unnamed x12, local copies, waits for them, and re-layouts  5.32 us

profile of v1, /device:TPU:1, one launch (start us, length us, event | category | flops | bytes accessed | tf_op | source)
XLA Modules:
  0.0 76.9 jit_solution(11598579782063318376)
XLA Ops:
  0.6 0.0 copy-start
  0.6 0.9 %copy-done = f32[2,3,4,8,256]{4,3,2,1,0:T(8,128)S(1)} copy-done((f32[2,3,4,8,256]{4,3,2,1,0:T(8,128)S(1)}, f32[2,3,4,8,256]{4,3,2,1,0:T(8,128)}, u32[]{:S(2)}) %copy-start) | copy-done | bytes 196632
  1.6 0.0 copy-start.1
  1.6 0.8 %copy-done.1 = s32[2,4,8,256]{3,2,1,0:T(8,128)S(1)} copy-done((s32[2,4,8,256]{3,2,1,0:T(8,128)S(1)}, s32[2,4,8,256]{3,2,1,0:T(8,128)}, u32[]{:S(2)}) %copy-start.1) | copy-done | bytes 65560
  2.4 0.0 copy-start.2
  2.4 0.8 copy-done.2
  3.2 0.0 copy-start.3
  3.2 0.8 copy-done.3
  3.9 0.0 copy-start.4
  3.9 0.8 copy-done.4
  4.7 70.4 %shard_map.76 = (f32[2,3,4,8,256]{4,3,2,1,0:T(8,128)S(1)}, f32[4,8,256]{2,1,0:T(8,128)S(1)}, f32[1,128]{1,0:T(1,128)S(1)}) custom-call(f32[4,8,256]{2,1,0:T(8,128)S(1)} %copy-done.2, s32[4,8,256]{2,1,0:T(8,128)S(1)} %copy-done.3, s32[4,8,256]{2,1,0:T(8,128)S(1)} %copy-done.4, s32[2,4,8,256]{3,2,1,0:T(8,128)S(1)} %copy-done.1, f32[2,3,4,8,256]{4,3,2,1,0:T(8,128)S(1)} %copy-done), custom_call_target="tpu_custom_call" | custom-call | tf_op jit(solution)/shard_map/pallas_call | solution.py:874
  75.1 0.5 slice_bitcast_fusion
  75.6 0.7 copy.10
  76.3 0.6 copy.11
Async XLA Ops:
  0.6 0.9 %copy-start = (f32[2,3,4,8,256]{4,3,2,1,0:T(8,128)S(1)}, f32[2,3,4,8,256]{4,3,2,1,0:T(8,128)}, u32[]{:S(2)}) copy-start(f32[2,3,4,8,256]{4,3,2,1,0:T(8,128)} %tra_in.1) | copy-start | bytes 589828
  1.6 0.8 %copy-start.1 = (s32[2,4,8,256]{3,2,1,0:T(8,128)S(1)}, s32[2,4,8,256]{3,2,1,0:T(8,128)}, u32[]{:S(2)}) copy-start(s32[2,4,8,256]{3,2,1,0:T(8,128)} %lod_in.1) | copy-start | bytes 196612
  2.4 0.8 copy-start.2
  3.2 0.8 copy-start.3
  3.9 0.8 copy-start.4

commit v2 on v1

--- a/solution.py
+++ b/solution.py
@@ -114,7 +114,7 @@
                         g_ref[tile, p, 4 * c + 2 * hy + hz] = g[r : r + 8, q : q + 128]
         return carry
 
-    lax.fori_loop(0, planes, body, 0)
+    lax.fori_loop(0, planes, body, 0, unroll=True)
 
 
 def tile_place(tile, lanes):
@@ -149,7 +149,7 @@
 
         start = tuple(g_ref[tile, 0, k] for k in range(12))
         zeros = tuple(jnp.zeros((8, 128), F32) for _ in range(12))
-        lax.fori_loop(0, elements, body, start + zeros)
+        lax.fori_loop(0, elements, body, start + zeros, unroll=True)
         return carry
 
     lax.fori_loop(0, tiles, over_tile, 0)
@@ -182,7 +182,7 @@
                 use(3 * l + c, e, gather_nodes(h_ref, e, c, z, lanes))
             return inner
 
-        lax.fori_loop(1, elements, nodes, 0)
+        lax.fori_loop(1, elements, nodes, 0, unroll=True)
         return carry
 
     lax.fori_loop(0, groups, one, 0)
@@ -244,24 +244,19 @@
 
 def kernel(dens, pas_in, sup_in, lod_in, tra_in, disp, sens, comp, *scratch):
     m = dict(zip(NAMES, scratch))
-    load_sem, send_sem, recv_sem, group_send, group_recv = scratch[len(NAMES) :]
+    load_sem, send_sem, recv_sem, group_send, group_recv, token = scratch[len(NAMES) :]
     gx, gy = lax.axis_index("gx"), lax.axis_index("gy")
-    me = gx * NY + gy
 
     def device(ax, ay):
         return lax.rem(gx + ax + NX, NX), lax.rem(gy + ay + NY, NY)
 
     barrier = pltpu.get_barrier_semaphore()
 
-    def greet(k, carry):
-        other = lax.rem(me + k, NX * NY)
+    around = [(a, b) for a in (-1, 0, 1) for b in (-1, 0, 1) if (a, b) != (0, 0)]
+    for ax, ay in around:
         pl.semaphore_signal(
-            barrier, inc=1, device_id=(other // NY, lax.rem(other, NY)),
-            device_id_type=pl.DeviceIdType.MESH,
+            barrier, inc=1, device_id=device(ax, ay), device_id_type=pl.DeviceIdType.MESH
         )
-        return carry
-
-    lax.fori_loop(1, NX * NY, greet, 0)
 
     loads = [
         pltpu.make_async_copy(dens, m["df"].at[pl.ds(4, 4)], load_sem.at[0]),
@@ -344,7 +339,7 @@
         m["yb_dn"][0, x, 7:8] = jnp.zeros((1, BZ), F32)
         m["yb_dn"][1, x, 7:8] = jnp.zeros((1, BZ), F32)
 
-    pl.semaphore_wait(barrier, NX * NY - 1)
+    pl.semaphore_wait(barrier, len(around))
 
     ra_lo, ra_hi, rb_lo, rb_hi = m["ra_lo"], m["ra_hi"], m["rb_lo"], m["rb_hi"]
     own = df.at[pl.ds(4, 4)]
@@ -384,7 +379,7 @@
         d16[p] = jnp.where(rows0 * here > 0.0, both, 0.0)
         return carry
 
-    lax.fori_loop(0, 12, put_density, 0)
+    lax.fori_loop(0, 12, put_density, 0, unroll=True)
 
     def stiffen(i, carry):
         x = gx * BX + i - 2
@@ -403,7 +398,7 @@
         m["coef"][i] = coef[0:8]
         return carry
 
-    lax.fori_loop(0, 8, stiffen, 0)
+    lax.fori_loop(0, 8, stiffen, 0, unroll=True)
 
     zi2, zo2 = iota((BZ, 128), 0), iota((BZ, 128), 1)
     pairs_z = inside(zi2 // 2 == zo2) * 0.125
@@ -457,7 +452,7 @@
             x0[f, p] = inv * b
         return carry
 
-    lax.fori_loop(0, 7, begin, 0)
+    lax.fori_loop(0, 7, begin, 0, unroll=True)
 
     def residual(f, e, image):
         m["r0"][f, e - 1] = keep[e, 0:8] * (b16[f, e, 0:8] - image[0:8])
@@ -474,7 +469,7 @@
         m["zl"][3 * f + 2] = 0.5 * r[3]
         return carry
 
-    lax.fori_loop(0, 6, rest_x, 0)
+    lax.fori_loop(0, 6, rest_x, 0, unroll=True)
     flat = mm(m["zl"][...].reshape(144, BZ), rest_z)
     m["zr"][...] = flat.reshape(18, 8, 128)
     pb, pbu, pbd = m["pb"], m["pbu"], m["pbd"]
@@ -490,7 +485,7 @@
             pb[f, i, 4:5] = 0.5 * v[7:8]
         return carry
 
-    lax.fori_loop(0, 6, rest_y, 0)
+    lax.fori_loop(0, 6, rest_y, 0, unroll=True)
 
     def pack_y(c, carry):
         for i in range(3):
@@ -502,7 +497,7 @@
             pbd[c, i] = jnp.where((sh >= 4) & (sh <= 6), turned, jnp.where(sh < 3, two, 0.0))
         return carry
 
-    lax.fori_loop(0, 3, pack_y, 0)
+    lax.fori_loop(0, 3, pack_y, 0, unroll=True)
 
     rd1, rd2, rp1, rp2 = m["rd1"], m["rd2"], m["rp1"], m["rp2"]
 
@@ -525,11 +520,12 @@
         message(pbu, rp1.at[1, 0], 0, 1),
         message(pbd, rp1.at[1, 1], 0, -1),
     ]
+    rs1 = m["rs1"]
+    group_done(rs1, group_recv, 0)
     for copy in third:
         copy.start()
 
-    rs1, s1, invd1 = m["rs1"], m["s1"], m["invd1"]
-    group_done(rs1, group_recv, 0)
+    s1, invd1 = m["s1"], m["invd1"]
     for p in range(8):
         x = p - 3
         dx, i = x // 2, x % 2
@@ -550,7 +546,7 @@
         invd1[p] = jnp.where(here > 0.0, (0.5 / (2.0 * DIAG)) / t, 0.0)
         return carry
 
-    lax.fori_loop(0, 7, diag1, 0)
+    lax.fori_loop(0, 7, diag1, 0, unroll=True)
 
     zi1, zo1 = iota((128, 128), 0), iota((128, 128), 1)
     pairs_2 = inside(zi1 // 2 == zo1 % 64) * 0.125
@@ -636,6 +632,10 @@
     rb2 = m["rb2"]
     group(lambda dx, dy: m["t2v"].at[dy % 4], rb2, R3_SLOTS, 1)
     group_done(rb2, group_recv, 1)
+    for ax in (-8, 8):
+        pl.semaphore_signal(
+            token, inc=1, device_id=device(ax, 0), device_id_type=pl.DeviceIdType.MESH
+        )
 
     s2, invd2, b2, x2 = m["s2"], m["invd2"], m["b2"], m["x2"]
     pair = sh // 2
@@ -695,7 +695,7 @@
             yy2[k, 15:16] = odd[15:16]
         return carry
 
-    lax.fori_loop(0, 4, widen_2, 0)
+    lax.fori_loop(0, 4, widen_2, 0, unroll=True)
     zi3, zo3 = iota((128, BZ), 0), iota((128, BZ), 1)
     near = jnp.abs(zo3 % 128 - 2 * (zi3 % 64))
     pro_2 = jnp.where(near == 0, 1.0, jnp.where(near == 1, 0.5, 0.0)).astype(F32)
@@ -737,7 +737,7 @@
         v1[at] = mm(yy1[at].reshape(80, 128), pro_1).reshape(5, 16, BZ)
         return carry
 
-    lax.fori_loop(0, 6, widen_z, 0)
+    lax.fori_loop(0, 6, widen_z, 0, unroll=True)
 
     def correct(f, carry):
         for p in range(7):
@@ -810,6 +810,7 @@
     for k in range(NY - 1):
         total = total + ry[k]
     sy[...] = total
+    pl.semaphore_wait(token, 2)
     group(lambda dx, dy: sy, rx, [(k, 0) for k in range(1, NX)], 3)
 
     for copy in fourth:
@@ -827,13 +828,13 @@
             f16[p] = jnp.where(here > 0.0, both, 0.0)
             return inner
 
-        lax.fori_loop(0, 8, put, 0)
+        lax.fori_loop(0, 8, put, 0, unroll=True)
 
         def run(x, inner):
             fil[l, x] = filter_plane(lambda p: f16[p], x + 2)[0:8]
             return inner
 
-        lax.fori_loop(0, 4, run, 0)
+        lax.fori_loop(0, 4, run, 0, unroll=True)
         return carry
 
     lax.fori_loop(0, 2, filter_load, 0)
@@ -878,10 +879,11 @@
             jax.ShapeDtypeStruct((BX, BY, BZ), F32),
             jax.ShapeDtypeStruct((1, 128), F32),
         ),
-        in_specs=[pl.BlockSpec(memory_space=pl.ANY)] * 5,
+        in_specs=[pl.BlockSpec(memory_space=pltpu.HBM)] * 5,
         out_specs=tuple(pl.BlockSpec(memory_space=pltpu.VMEM) for _ in range(3)),
         scratch_shapes=scratch
-        + [dma((5,)), dma((N_SEMS,)), dma((N_SEMS,)), dma((4,)), dma((4,))],
+        + [dma((5,)), dma((N_SEMS,)), dma((N_SEMS,)), dma((4,)), dma((4,))]
+        + [pltpu.SemaphoreType.REGULAR],
         compiler_params=pltpu.CompilerParams(
             collective_id=0, has_side_effects=True, vmem_limit_bytes=40 * 2**20
         ),

time: 77.2 us -> 61.8 us (0.80)
  Pallas kernels: 70.4 us -> 55 us
    pallas_call x1, Pallas kernels: 70.4 us -> 55 us  [per_device(): pl.pallas_call(kernel, out_shape=(jax.ShapeDtypeStruct((2, 3, BX, BY, BZ)...]
where the time goes in v2:
time: 61.8 us; the launch traced here: 61.5 us
  Pallas kernels  55 us (89%)
  local copies, waits for them, and re-layouts  5.83 us (9%)
  between operations  0.65 us (1%)
    pallas_call x1, Pallas kernels, per_device(): pl.pallas_call(kernel, out_shape=(jax.ShapeDtypeStruct((2, 3, BX, BY, BZ)...  55 us
    unnamed x12, local copies, waits for them, and re-layouts  5.32 us

profile of v2, /device:TPU:1, one launch (start us, length us, event | category | flops | bytes accessed | tf_op | source)
XLA Modules:
  0.0 61.5 jit_solution(10073512733129883455)
XLA Ops:
  0.6 0.0 copy-start
  0.6 0.9 %copy-done = f32[2,3,4,8,256]{4,3,2,1,0:T(8,128)S(1)} copy-done((f32[2,3,4,8,256]{4,3,2,1,0:T(8,128)S(1)}, f32[2,3,4,8,256]{4,3,2,1,0:T(8,128)}, u32[]{:S(2)}) %copy-start) | copy-done | bytes 196632
  1.6 0.0 copy-start.1
  1.6 0.8 %copy-done.1 = s32[2,4,8,256]{3,2,1,0:T(8,128)S(1)} copy-done((s32[2,4,8,256]{3,2,1,0:T(8,128)S(1)}, s32[2,4,8,256]{3,2,1,0:T(8,128)}, u32[]{:S(2)}) %copy-start.1) | copy-done | bytes 65560
  2.4 0.0 copy-start.2
  2.4 0.8 %copy-done.2 = f32[4,8,256]{2,1,0:T(8,128)S(1)} copy-done((f32[4,8,256]{2,1,0:T(8,128)S(1)}, f32[4,8,256]{2,1,0:T(8,128)}, u32[]{:S(2)}) %copy-start.2) | copy-done | bytes 32792
  3.2 0.0 copy-start.3
  3.2 0.8 %copy-done.3 = s32[4,8,256]{2,1,0:T(8,128)S(1)} copy-done((s32[4,8,256]{2,1,0:T(8,128)S(1)}, s32[4,8,256]{2,1,0:T(8,128)}, u32[]{:S(2)}) %copy-start.3) | copy-done | bytes 32792
  3.9 0.0 copy-start.4
  3.9 0.8 %copy-done.4 = s32[4,8,256]{2,1,0:T(8,128)S(1)} copy-done((s32[4,8,256]{2,1,0:T(8,128)S(1)}, s32[4,8,256]{2,1,0:T(8,128)}, u32[]{:S(2)}) %copy-start.4) | copy-done | bytes 32792
  4.7 55.0 %shard_map.76 = (f32[2,3,4,8,256]{4,3,2,1,0:T(8,128)S(1)}, f32[4,8,256]{2,1,0:T(8,128)S(1)}, f32[1,128]{1,0:T(1,128)S(1)}) custom-call(f32[4,8,256]{2,1,0:T(8,128)S(1)} %copy-done.2, s32[4,8,256]{2,1,0:T(8,128)S(1)} %copy-done.3, s32[4,8,256]{2,1,0:T(8,128)S(1)} %copy-done.4, s32[2,4,8,256]{3,2,1,0:T(8,128)S(1)} %copy-done.1, f32[2,3,4,8,256]{4,3,2,1,0:T(8,128)S(1)} %copy-done), custom_call_target="tpu_custom_call" | custom-call | tf_op jit(solution)/shard_map/pallas_call | solution.py:875
  59.7 0.5 slice_bitcast_fusion
  60.2 0.7 %copy.10 = f32[2,3,4,8,256]{4,3,2,1,0:T(8,128)} copy(f32[2,3,4,8,256]{4,3,2,1,0:T(8,128)S(1)} %get-tuple-element.12) | data formatting | bytes 393216
  60.9 0.6 copy.11
Async XLA Ops:
  0.6 0.9 %copy-start = (f32[2,3,4,8,256]{4,3,2,1,0:T(8,128)S(1)}, f32[2,3,4,8,256]{4,3,2,1,0:T(8,128)}, u32[]{:S(2)}) copy-start(f32[2,3,4,8,256]{4,3,2,1,0:T(8,128)} %tra_in.1) | copy-start | bytes 589828
  1.6 0.8 %copy-start.1 = (s32[2,4,8,256]{3,2,1,0:T(8,128)S(1)}, s32[2,4,8,256]{3,2,1,0:T(8,128)}, u32[]{:S(2)}) copy-start(s32[2,4,8,256]{3,2,1,0:T(8,128)} %lod_in.1) | copy-start | bytes 196612
  2.4 0.8 %copy-start.2 = (f32[4,8,256]{2,1,0:T(8,128)S(1)}, f32[4,8,256]{2,1,0:T(8,128)}, u32[]{:S(2)}) copy-start(f32[4,8,256]{2,1,0:T(8,128)} %dens.1) | copy-start | bytes 98308
  3.2 0.8 %copy-start.3 = (s32[4,8,256]{2,1,0:T(8,128)S(1)}, s32[4,8,256]{2,1,0:T(8,128)}, u32[]{:S(2)}) copy-start(s32[4,8,256]{2,1,0:T(8,128)} %pas_in.1) | copy-start | bytes 98308
  3.9 0.8 %copy-start.4 = (s32[4,8,256]{2,1,0:T(8,128)S(1)}, s32[4,8,256]{2,1,0:T(8,128)}, u32[]{:S(2)}) copy-start(s32[4,8,256]{2,1,0:T(8,128)} %sup_in.1) | copy-start | bytes 98308

commit v3 on v2

--- a/solution.py
+++ b/solution.py
@@ -19,7 +19,20 @@
 DIAG = (LAME1 + 4.0 * LAME2) / 9.0
 EDGE = math.tanh(4.0)
 
+
+def far(slot):
+    dx, dy = slot
+    hops = 0
+    for x in range(4):
+        ring = abs((x + dx) % 4 - x)
+        hops += min(ring, 4 - ring) + abs((x + dx) // 4)
+    for core in range(2):
+        hops += 2 * abs((core + dy) // 2)
+    return -hops
+
+
 R3_SLOTS = [(a, b) for a in range(-4, 6) for b in range(-2, 4) if (a, b) != (0, 0)]
+R3_SLOTS.sort(key=far)
 S1_SLOTS = [(a, b) for a in range(-2, 3) for b in range(-1, 2) if (a, b) != (0, 0)]
 
 
@@ -223,17 +236,17 @@
     b16=(6, 7, 16, BZ), x0=(6, 7, 16, BZ), keep=(7, 16, BZ), invd=(7, 16, BZ),
     g=(4, 7, 12, 8, 128), h=(4, 6, 12, 8, 128), r0=(6, 4, 8, BZ),
     zl=(18, 8, BZ), zr=(18, 8, 128), zc=(2, 8, 128),
-    pb=(6, 3, 8, 128), pbu=(3, 3, 8, 128), pbd=(3, 3, 8, 128),
+    pb=(6, 3, 8, 128), pbp=(4, 3, 8, 128), pbu=(3, 3, 8, 128), pbd=(3, 8, 128),
+    pbe=(3, 3, 8, 128),
     s1s=(2, 8, 128), rs1=(len(S1_SLOTS), 2, 8, 128),
-    rd1=(2, 6, 3, 8, 128), rd2=(2, 6, 1, 8, 128),
-    rp1=(3, 2, 3, 3, 8, 128), rp2=(2, 2, 3, 1, 8, 128),
+    rp=(5, 4, 3, 8, 128), ru=(5, 3, 3, 8, 128), rd=(5, 3, 8, 128), re=(5, 3, 3, 8, 128),
     s1=(8, 16, 128), invd1=(7, 16, 128), b1=(6, 7, 16, 128), x1=(6, 7, 16, 128),
     g1=(2, 7, 12, 8, 128), h1=(2, 6, 12, 8, 128), r1=(6, 3, 16, 128),
     t2l=(4, 8, BZ), t2r=(4, 8, 128), t2=(8, 128), t2v=(4, 8, 128), rb2=(len(R3_SLOTS), 8, 128),
     s2=(10, 16, 128), invd2=(10, 16, 128), b2=(3, 10, 16, 128), x2=(3, 10, 16, 128),
     g2=(2, 10, 12, 8, 128), h2=(2, 9, 12, 8, 128),
     yy2=(12, 16, 128), w2=(12, 16, BZ), yy1=(30, 16, 128), v1=(30, 16, BZ),
-    sums=(8, 128), ry=(7, 8, 128), sy=(8, 128), rx=(31, 8, 128),
+    sums=(1, 128), rc=(1, 128), sc=(1, 128), rx=(127, 1, 128),
     rt=(2, 8, 8, BZ), yt=(4, 8, BZ), rt_lo=(8, 8, BZ), rt_hi=(8, 8, BZ),
     f16=(8, 16, BZ), fil=(2, 4, 8, BZ),
 )
@@ -242,9 +255,9 @@
 N_SEMS = 64
 
 
-def kernel(dens, pas_in, sup_in, lod_in, tra_in, disp, sens, comp, *scratch):
+def kernel(dens, pas_in, sup_in, lod_in, tra_in, pre_out, fil_out, scal_out, *scratch):
     m = dict(zip(NAMES, scratch))
-    load_sem, send_sem, recv_sem, group_send, group_recv, token = scratch[len(NAMES) :]
+    load_sem, send_sem, recv_sem, group_send, group_recv, out_sem, token = scratch[len(NAMES) :]
     gx, gy = lax.axis_index("gx"), lax.axis_index("gy")
 
     def device(ax, ay):
@@ -472,7 +485,7 @@
     lax.fori_loop(0, 6, rest_x, 0, unroll=True)
     flat = mm(m["zl"][...].reshape(144, BZ), rest_z)
     m["zr"][...] = flat.reshape(18, 8, 128)
-    pb, pbu, pbd = m["pb"], m["pbu"], m["pbd"]
+    pb, pbp, pbu, pbd, pbe = m["pb"], m["pbp"], m["pbu"], m["pbd"], m["pbe"]
     sh = sub(128)
 
     def rest_y(f, carry):
@@ -487,43 +500,53 @@
 
     lax.fori_loop(0, 6, rest_y, 0, unroll=True)
 
-    def pack_y(c, carry):
-        for i in range(3):
+    for i in range(3):
+        for c in range(3):
             one, two = pb[c, i], pb[3 + c, i]
             turned = y_down(one, 4)
             pbu[c, i] = jnp.where(
                 (sh >= 6) | (sh == 0), turned, jnp.where((sh >= 2) & (sh <= 4), two, 0.0)
             )
-            pbd[c, i] = jnp.where((sh >= 4) & (sh <= 6), turned, jnp.where(sh < 3, two, 0.0))
-        return carry
-
-    lax.fori_loop(0, 3, pack_y, 0, unroll=True)
-
-    rd1, rd2, rp1, rp2 = m["rd1"], m["rd2"], m["rp1"], m["rp2"]
-
-    def part(ref, lo, n):
-        return ref.at[:, pl.ds(lo, n)]
-
-    third = [
-        message(part(pbu, 2, 1), rp2.at[0, 0], 2, 1),
-        message(part(pbd, 2, 1), rp2.at[0, 1], 2, -1),
-        message(part(pb, 2, 1), rd2.at[0], 2, 0),
-        message(part(pbu, 0, 1), rp2.at[1, 0], -2, 1),
-        message(part(pbd, 0, 1), rp2.at[1, 1], -2, -1),
-        message(part(pb, 0, 1), rd2.at[1], -2, 0),
-        message(pbu, rp1.at[0, 0], 1, 1),
-        message(pbd, rp1.at[0, 1], 1, -1),
-        message(pb, rd1.at[0], 1, 0),
-        message(pbu, rp1.at[2, 0], -1, 1),
-        message(pbd, rp1.at[2, 1], -1, -1),
-        message(pb, rd1.at[1], -1, 0),
-        message(pbu, rp1.at[1, 0], 0, 1),
-        message(pbd, rp1.at[1, 1], 0, -1),
-    ]
+            pbe[c, i] = jnp.where(
+                (sh == 5) | (sh == 6), turned, jnp.where((sh == 1) | (sh == 2), two, 0.0)
+            )
+        for k in range(4):
+            rest = y_down(pb[4 + k // 2, i], 5 - 3 * (k % 2))
+            pbp[k, i] = jnp.where(sh < 5, pb[k, i], rest)
+        for f in range(6):
+            pbd[i, f : f + 1] = pb[f, i, 0:1]
+        pbd[i, 6:8] = jnp.zeros((2, 128), F32)
+
+    rp, ru, rd, re = m["rp"], m["ru"], m["rd"], m["re"]
+
+    def shares(ax, ay, lo, n):
+        slot, at = 2 - ax, pl.ds(lo, n)
+        if ay == 0:
+            return message(pbp.at[:, at], rp.at[slot, :, at], ax, 0)
+        if ay == 1:
+            return message(pbu.at[:, at], ru.at[slot, :, at], ax, 1)
+        return message(pbd.at[at], rd.at[slot, at], ax, -1)
+
+    def late_rows(ax, lo, n):
+        slot, at = 2 - ax, pl.ds(lo, n)
+        return message(pbe.at[:, at], re.at[slot, :, at], ax, -1)
+
+    third = [shares(2, ay, 2, 1) for ay in (1, -1, 0)]
+    third += [shares(1, ay, 0, 3) for ay in (1, -1, 0)]
+    third += [shares(-1, ay, 0, 1) for ay in (1, -1, 0)]
+    third += [shares(0, 1, 0, 3), shares(0, -1, 0, 3)]
+    late = [shares(-1, ay, 1, 2) for ay in (1, -1, 0)]
+    late += [shares(-2, ay, 0, 1) for ay in (1, -1, 0)]
+    late += [late_rows(1, 0, 3), late_rows(2, 2, 1), late_rows(0, 0, 3)]
+    late += [late_rows(-1, 0, 3), late_rows(-2, 0, 1)]
+    for copy in third + late:
+        copy.start()
+
     rs1 = m["rs1"]
     group_done(rs1, group_recv, 0)
-    for copy in third:
-        copy.start()
+    pl.semaphore_signal(
+        token.at[0], inc=1, device_id=device(2, 0), device_id_type=pl.DeviceIdType.MESH
+    )
 
     s1, invd1 = m["s1"], m["invd1"]
     for p in range(8):
@@ -568,42 +591,49 @@
     okx = {d: (gx + d >= 0) & (gx + d < NX) for d in range(-2, 3)}
     oky = {d: (gy + d >= 0) & (gy + d < NY) for d in range(-1, 2)}
 
-    def share(dx, dy, index, i):
-        if dx == 0 and dy == 0:
-            return pb[index, i]
-        if dy == 0:
-            v = rd1[0 if dx < 0 else 1, index, i] if abs(dx) == 1 else rd2[0 if dx < 0 else 1, index, 0]
-        else:
-            k = 0 if dy < 0 else 1
-            v = rp1[dx + 1, k, index, i] if abs(dx) < 2 else rp2[0 if dx < 0 else 1, k, index, 0]
-        return jnp.where(okx[dx] & oky[dy], v, 0.0)
-
     def sources(x):
-        return [(dx, x - 2 * dx) for dx in range(-2, 3) if 0 <= x - 2 * dx <= 2 and (abs(dx) < 2 or (dx, x) in ((-2, -2), (2, 4)))]
-
-    def right_side_1(c, carry):
-        for p in range(7):
+        return [(dx, x - 2 * dx) for dx in range(-2, 3) if 0 <= x - 2 * dx <= 2]
+
+    def summed(x, dy, read):
+        total = None
+        for dx, i in sources(x):
+            if (dx, dy) != (0, 0):
+                v = jnp.where(okx[dx] & oky[dy], read(dx + 2, i), 0.0)
+                total = v if total is None else total + v
+        return total
+
+    def right_side_1(planes, whole):
+        for p in planes:
             x = p - 2
-            up = down = None
-            for dx, i in sources(x):
-                u, d = share(dx, -1, c, i), share(dx, 1, c, i)
-                up = u if up is None else up + u
-                down = d if down is None else down + d
-            for l in range(2):
-                mid = None
-                for dx, i in sources(x):
-                    v = share(dx, 0, 3 * l + c, i)
-                    mid = v if mid is None else mid + v
-                if l == 1:
-                    up, down = y_down(up, 4), y_down(down, 4)
-                tile0 = mid + jnp.where(sh == 0, up, jnp.where((sh >= 4) & (sh <= 6), down, 0.0))
-                tile1 = jnp.where(sh >= 6, up, 0.0)
-                v = jnp.concatenate([tile0, tile1], axis=0)
-                b1[3 * l + c, p] = v
-                x1[3 * l + c, p] = invd1[p] * v
-        return carry
-
-    lax.fori_loop(0, 3, right_side_1, 0)
+            mids = [summed(x, 0, lambda d, i, k=k: rp[d, k, i]) for k in range(4)]
+            if mids[0] is not None:
+                mids = [jnp.where(sh < 5, v, 0.0) for v in mids] + [
+                    jnp.where(
+                        sh < 3, y_down(mids[k], 3), jnp.where(sh < 5, y_up(mids[k + 1], 2), 0.0)
+                    )
+                    for k in (0, 2)
+                ]
+            line4 = summed(x, 1, lambda d, i: rd[d, i])
+            for c in range(3):
+                up = summed(x, -1, lambda d, i, c=c: ru[d, c, i])
+                ends = summed(x, 1, lambda d, i, c=c: re[d, c, i]) if whole else None
+                for l in range(2):
+                    f = 3 * l + c
+                    if l == 1:
+                        up = y_down(up, 4)
+                        ends = y_down(ends, 4) if whole else None
+                    t0 = jnp.where(sh == 0, up, jnp.where(sh == 4, line4[f : f + 1], 0.0))
+                    if whole:
+                        t0 = jnp.where((sh == 5) | (sh == 6), ends, t0)
+                    if 0 <= x <= 2:
+                        t0 = t0 + pb[f, x]
+                    if mids[0] is not None:
+                        t0 = t0 + mids[f]
+                    v = jnp.concatenate([t0, jnp.where(sh >= 6, up, 0.0)], axis=0)
+                    b1[f, p] = v
+                    x1[f, p] = invd1[p] * v
+
+    right_side_1(range(5), False)
 
     def residual_1(f, e, image):
         m["r1"][f, e - 1] = b1[f, e] - image
@@ -630,11 +660,15 @@
         m["t2v"][k] = t2[...] if k == 0 else y_down(t2[...], 2 * k)
 
     rb2 = m["rb2"]
+    pl.semaphore_wait(token.at[0], 1)
     group(lambda dx, dy: m["t2v"].at[dy % 4], rb2, R3_SLOTS, 1)
+    for copy in late:
+        copy.wait_recv()
+    right_side_1(range(7), True)
     group_done(rb2, group_recv, 1)
     for ax in (-8, 8):
         pl.semaphore_signal(
-            token, inc=1, device_id=device(ax, 0), device_id_type=pl.DeviceIdType.MESH
+            token.at[1], inc=1, device_id=device(ax, 0), device_id_type=pl.DeviceIdType.MESH
         )
 
     s2, invd2, b2, x2 = m["s2"], m["invd2"], m["b2"], m["x2"]
@@ -754,8 +788,18 @@
 
     apply_level(x0, 2, 0, s16, 1, 1.0, 6, m["g"], m["h"], BZ, BZ, smooth_0)
 
+    outs = [
+        pltpu.make_async_copy(
+            x0.at[pl.ds(3 * l, 3), pl.ds(1, 4), pl.ds(0, 8)], pre_out.at[l], out_sem.at[l]
+        )
+        for l in range(2)
+    ]
+    for copy in outs:
+        copy.start()
+
     rt, yt, sums = m["rt"], m["yt"], m["sums"]
-    sums[...] = jnp.zeros((8, 128), F32)
+    sums[...] = jnp.zeros((1, 128), F32)
+    line = iota((1, 128), 1)
 
     def energies(l, carry):
         spread_planes(x0, 3 * l, 1, 5, m["g"], BZ, 2)
@@ -778,14 +822,19 @@
                 rt[l, 2 + e, :, q] = energy * m["coef"][2 + e, :, q]
                 for c in range(3):
                     dot = dot + b16[3 * l + c, 1 + e, 0:8, q] * x0[3 * l + c, 1 + e, 0:8, q]
-        sums[pl.ds(l, 1)] = jnp.sum(dot, axis=0, keepdims=True)
-        sums[pl.ds(2 + l, 1)] = jnp.sum(curve, axis=0, keepdims=True)
+        for k, v in ((l, dot), (2 + l, curve)):
+            v = jnp.sum(jnp.sum(v, axis=0, keepdims=True), axis=1, keepdims=True)
+            sums[...] = jnp.where(line == k, v, sums[...])
         return carry
 
     lax.fori_loop(0, 2, energies, 0)
 
-    ry, sy, rx = m["ry"], m["sy"], m["rx"]
-    group(lambda dx, dy: sums, ry, [(0, k) for k in range(1, NY)], 2)
+    rc, sc, rx = m["rc"], m["sc"], m["rx"]
+    twin = pltpu.make_async_remote_copy(
+        src_ref=sums, dst_ref=rc, send_sem=group_send.at[2], recv_sem=group_recv.at[2],
+        device_id=(gx, gy + 1 - 2 * lax.rem(gy, 2)), device_id_type=pl.DeviceIdType.MESH,
+    )
+    twin.start()
     for x in range(4):
         one, two = rt[0, 2 + x], rt[1, 2 + x]
         yt[x] = jnp.where(
@@ -805,13 +854,24 @@
     ]
     for copy in fourth:
         copy.start()
-    group_done(ry, group_recv, 2)
-    total = sums[...]
-    for k in range(NY - 1):
-        total = total + ry[k]
-    sy[...] = total
-    pl.semaphore_wait(token, 2)
-    group(lambda dx, dy: sy, rx, [(k, 0) for k in range(1, NX)], 3)
+    pl.semaphore_wait(token.at[1], 2)
+    twin.wait_recv()
+    sc[...] = sums[...] + rc[...]
+
+    def tell(k, ax, ay):
+        pltpu.make_async_remote_copy(
+            src_ref=sc, dst_ref=rx.at[k], send_sem=group_send.at[3],
+            recv_sem=group_recv.at[3], device_id=(lax.rem(gx + ax, NX), lax.rem(gy + ay, NY)),
+            device_id_type=pl.DeviceIdType.MESH,
+        ).start()
+
+    def tell_far(k, carry):
+        tell(k, 1 + lax.rem(k // 4 + 13, NX - 1), 2 * lax.rem(k, 4))
+        return carry
+
+    lax.fori_loop(0, 4 * (NX - 1), tell_far, 0)
+    for k in range(3):
+        tell(4 * (NX - 1) + k, 0, 2 + 2 * k)
 
     for copy in fourth:
         copy.wait_recv()
@@ -839,32 +899,33 @@
 
     lax.fori_loop(0, 2, filter_load, 0)
 
+    outs.append(pltpu.make_async_copy(fil, fil_out, out_sem.at[2]))
+    outs[2].start()
     group_done(rx, group_recv, 3)
-    total = sy[...]
-    for k in range(NX - 1):
-        total = total + rx[k]
-    total = jnp.sum(total, axis=1, keepdims=True)
-    steps = []
-    line = iota((1, 128), 1)
+    total = sc[...] + jnp.sum(rx[...], axis=0)
     out = jnp.zeros((1, 128), F32)
     for l in range(2):
-        dot, curve = total[l : l + 1], total[2 + l : 3 + l]
+        dot, curve = total[:, l : l + 1], total[:, 2 + l : 3 + l]
         step = dot / curve
-        steps.append(step)
-        out = jnp.where(line == l, step * dot * (1.0 / CELLS), out)
-    comp[...] = out
-    for x in range(4):
-        sens[x] = fil[0, x] * (steps[0] * steps[0]) + fil[1, x] * (steps[1] * steps[1])
-        for l in range(2):
-            for c in range(3):
-                disp[l, c, x] = x0[3 * l + c, 1 + x, 0:8] * steps[l]
-
-    for copy in first + second + third + fourth:
+        for k, v in ((l, step * dot * (1.0 / CELLS)), (2 + l, step), (4 + l, step * step)):
+            out = jnp.where(line == k, v, out)
+    scal_out[...] = out
+    for copy in outs:
+        copy.wait()
+
+    for copy in first + second + third + late + fourth:
         copy.wait_send()
     group_done(m["rs1"], group_send, 0)
     group_done(rb2, group_send, 1)
-    group_done(ry, group_send, 2)
+    twin.wait_send()
     group_done(rx, group_send, 3)
+
+
+def scale_kernel(precond, filtered, scalars, disp, sens, comp):
+    for l in range(2):
+        comp[l] = scalars[0, l]
+        disp[l] = precond[l] * scalars[0, 2 + l]
+    sens[...] = filtered[0] * scalars[0, 4] + filtered[1] * scalars[0, 5]
 
 
 def per_device(density, passive_void_mask, support_node_mask, loaded_node_mask, traction):
@@ -872,23 +933,35 @@
         pltpu.VMEM(shape, jnp.int32 if name in INTS else F32) for name, shape in SCRATCH.items()
     ]
     dma = pltpu.SemaphoreType.DMA
-    displacement, sensitivity, compliance = pl.pallas_call(
+    hbm = pl.BlockSpec(memory_space=pltpu.HBM)
+    precond, filtered, scalars = pl.pallas_call(
         kernel,
         out_shape=(
             jax.ShapeDtypeStruct((2, 3, BX, BY, BZ), F32),
-            jax.ShapeDtypeStruct((BX, BY, BZ), F32),
+            jax.ShapeDtypeStruct((2, BX, BY, BZ), F32),
             jax.ShapeDtypeStruct((1, 128), F32),
         ),
-        in_specs=[pl.BlockSpec(memory_space=pltpu.HBM)] * 5,
-        out_specs=tuple(pl.BlockSpec(memory_space=pltpu.VMEM) for _ in range(3)),
+        in_specs=[hbm] * 5,
+        out_specs=(hbm, hbm, pl.BlockSpec(memory_space=pltpu.VMEM)),
         scratch_shapes=scratch
         + [dma((5,)), dma((N_SEMS,)), dma((N_SEMS,)), dma((4,)), dma((4,))]
-        + [pltpu.SemaphoreType.REGULAR],
+        + [dma((3,)), pltpu.SemaphoreType.REGULAR((2,))],
         compiler_params=pltpu.CompilerParams(
-            collective_id=0, has_side_effects=True, vmem_limit_bytes=40 * 2**20
+            collective_id=0, has_side_effects=True, vmem_limit_bytes=63 * 2**20
         ),
     )(density, passive_void_mask, support_node_mask, loaded_node_mask, traction)
-    return displacement, sensitivity, compliance[0, :2]
+    vmem, smem = pl.BlockSpec(memory_space=pltpu.VMEM), pl.BlockSpec(memory_space=pltpu.SMEM)
+    return pl.pallas_call(
+        scale_kernel,
+        out_shape=(
+            jax.ShapeDtypeStruct((2, 3, BX, BY, BZ), F32),
+            jax.ShapeDtypeStruct((BX, BY, BZ), F32),
+            jax.ShapeDtypeStruct((2,), F32),
+        ),
+        in_specs=[vmem, vmem, smem],
+        out_specs=(vmem, vmem, smem),
+        compiler_params=pltpu.CompilerParams(vmem_limit_bytes=63 * 2**20),
+    )(precond, filtered, scalars)
 
 
 def solution(mesh):

time: 61.8 us -> 56 us (0.906)
  local copies, waits for them, and re-layouts: 5.83 us -> 0 us
    unnamed x12 -> x0, local copies, waits for them, and re-layouts: 5.32 us -> none
    pallas_call x0 -> x1, Pallas kernels: none -> 1.65 us  [per_device(): pl.pallas_call(scale_kernel, out_shape=(jax.ShapeDtypeStruct((2, 3, BX, B...]
    pallas_call x1, Pallas kernels: 55 us -> 53.6 us  [per_device(): pl.pallas_call(kernel, out_shape=(jax.ShapeDtypeStruct((2, 3, BX, BY, BZ)...]
where the time goes in v3:
time: 56 us; the launch traced here: 55.9 us
  Pallas kernels  55.3 us (99%)
  between operations  0.64 us (1%)
    pallas_call x1, Pallas kernels, per_device(): pl.pallas_call(kernel, out_shape=(jax.ShapeDtypeStruct((2, 3, BX, BY, BZ)...  53.6 us
    pallas_call x1, Pallas kernels, per_device(): pl.pallas_call(scale_kernel, out_shape=(jax.ShapeDtypeStruct((2, 3, BX, B...  1.65 us

profile of v3, /device:TPU:1, one launch (start us, length us, event | category | flops | bytes accessed | tf_op | source)
XLA Modules:
  0.0 55.9 jit_solution(9338648197328058977)
XLA Ops:
  0.6 53.6 %shard_map.76 = (f32[2,3,4,8,256]{4,3,2,1,0:T(8,128)}, f32[2,4,8,256]{3,2,1,0:T(8,128)}, f32[1,128]{1,0:T(1,128)}) custom-call(f32[4,8,256]{2,1,0:T(8,128)} %dens.1, s32[4,8,256]{2,1,0:T(8,128)} %pas_in.1, s32[4,8,256]{2,1,0:T(8,128)} %sup_in.1, s32[2,4,8,256]{3,2,1,0:T(8,128)} %lod_in.1, f32[2,3,4,8,256]{4,3,2,1,0:T(8,128)} %tra_in.1), custom_call_target="tpu_custom_call" | custom-call | tf_op jit(solution)/shard_map/pallas_call | solution.py:937
  54.2 1.7 %shard_map.77 = (f32[2,3,4,8,256]{4,3,2,1,0:T(8,128)}, f32[4,8,256]{2,1,0:T(8,128)}, f32[2]{0:T(128)}) custom-call(f32[2,3,4,8,256]{4,3,2,1,0:T(8,128)} %get-tuple-element.6.precond, f32[2,4,8,256]{3,2,1,0:T(8,128)} %get-tuple-element.7.filtered, f32[1,128]{1,0:T(1,128)} %get-tuple-element.8.scalars), custom_call_target="tpu_custom_call" | custom-call | tf_op jit(solution)/shard_map/pallas_call | solution.py:954

commit v4 on v3

--- a/solution.py
+++ b/solution.py
@@ -165,7 +165,7 @@
         lax.fori_loop(0, elements, body, start + zeros, unroll=True)
         return carry
 
-    lax.fori_loop(0, tiles, over_tile, 0)
+    lax.fori_loop(0, tiles, over_tile, 0, unroll=True)
 
 
 def gather_nodes(h_ref, e, c, z, lanes):
@@ -187,18 +187,18 @@
     tiles = 2 * lanes // 128
 
     def one(l, carry):
-        spread_planes(x_ref, 3 * l, xoff, elements + 1, g_ref, z, tiles)
-        element_planes(g_ref, h_ref, s_ref, soff, scale, elements, tiles, lanes)
+        spread_planes(x_ref, 3 * l, xoff, elements + 1, g_ref.at[l], z, tiles)
+        element_planes(g_ref.at[l], h_ref.at[l], s_ref, soff, scale, elements, tiles, lanes)
 
         def nodes(e, inner):
             for c in range(3):
-                use(3 * l + c, e, gather_nodes(h_ref, e, c, z, lanes))
+                use(3 * l + c, e, gather_nodes(h_ref.at[l], e, c, z, lanes))
             return inner
 
         lax.fori_loop(1, elements, nodes, 0, unroll=True)
         return carry
 
-    lax.fori_loop(0, groups, one, 0)
+    lax.fori_loop(0, groups, one, 0, unroll=True)
 
 
 def filter_plane(load, p):
@@ -234,17 +234,17 @@
     ra_lo=(12, 8, BZ), ra_hi=(12, 8, BZ), rb_lo=(7, 8, BZ), rb_hi=(2, 7, 8, BZ),
     gden=(3, 16, BZ), d16=(12, 16, BZ), s16=(8, 16, BZ), coef=(8, 8, BZ),
     b16=(6, 7, 16, BZ), x0=(6, 7, 16, BZ), keep=(7, 16, BZ), invd=(7, 16, BZ),
-    g=(4, 7, 12, 8, 128), h=(4, 6, 12, 8, 128), r0=(6, 4, 8, BZ),
+    g=(2, 4, 7, 12, 8, 128), h=(2, 4, 6, 12, 8, 128), r0=(6, 4, 8, BZ),
     zl=(18, 8, BZ), zr=(18, 8, 128), zc=(2, 8, 128),
     pb=(6, 3, 8, 128), pbp=(4, 3, 8, 128), pbu=(3, 3, 8, 128), pbd=(3, 8, 128),
     pbe=(3, 3, 8, 128),
     s1s=(2, 8, 128), rs1=(len(S1_SLOTS), 2, 8, 128),
     rp=(5, 4, 3, 8, 128), ru=(5, 3, 3, 8, 128), rd=(5, 3, 8, 128), re=(5, 3, 3, 8, 128),
     s1=(8, 16, 128), invd1=(7, 16, 128), b1=(6, 7, 16, 128), x1=(6, 7, 16, 128),
-    g1=(2, 7, 12, 8, 128), h1=(2, 6, 12, 8, 128), r1=(6, 3, 16, 128),
+    g1=(2, 2, 7, 12, 8, 128), h1=(2, 2, 6, 12, 8, 128), r1=(6, 3, 16, 128),
     t2l=(4, 8, BZ), t2r=(4, 8, 128), t2=(8, 128), t2v=(4, 8, 128), rb2=(len(R3_SLOTS), 8, 128),
     s2=(10, 16, 128), invd2=(10, 16, 128), b2=(3, 10, 16, 128), x2=(3, 10, 16, 128),
-    g2=(2, 10, 12, 8, 128), h2=(2, 9, 12, 8, 128),
+    g2=(1, 2, 10, 12, 8, 128), h2=(1, 2, 9, 12, 8, 128),
     yy2=(12, 16, 128), w2=(12, 16, BZ), yy1=(30, 16, 128), v1=(30, 16, BZ),
     sums=(1, 128), rc=(1, 128), sc=(1, 128), rx=(127, 1, 128),
     rt=(2, 8, 8, BZ), yt=(4, 8, BZ), rt_lo=(8, 8, BZ), rt_hi=(8, 8, BZ),
@@ -435,10 +435,10 @@
     def group_done(dst, sem, k):
         pltpu.make_async_copy(dst, dst, sem.at[k]).wait()
 
-    group(lambda dx, dy: m["s1s"], m["rs1"], S1_SLOTS, 0)
-
     for copy in second:
         copy.wait_recv()
+    group(lambda dx, dy: m["s1s"], m["rs1"], S1_SLOTS, 0)
+
 
     x0, b16, keep, invd = m["x0"], m["b16"], m["keep"], m["invd"]
 
@@ -531,8 +531,8 @@
         slot, at = 2 - ax, pl.ds(lo, n)
         return message(pbe.at[:, at], re.at[slot, :, at], ax, -1)
 
-    third = [shares(2, ay, 2, 1) for ay in (1, -1, 0)]
-    third += [shares(1, ay, 0, 3) for ay in (1, -1, 0)]
+    third = [shares(1, ay, 0, 3) for ay in (1, -1, 0)]
+    third += [shares(2, ay, 2, 1) for ay in (1, -1, 0)]
     third += [shares(-1, ay, 0, 1) for ay in (1, -1, 0)]
     third += [shares(0, 1, 0, 3), shares(0, -1, 0, 3)]
     late = [shares(-1, ay, 1, 2) for ay in (1, -1, 0)]
@@ -762,7 +762,7 @@
             yy1[k, 15:16] = odd[15:16]
         return carry
 
-    lax.fori_loop(0, 6, widen_1, 0)
+    lax.fori_loop(0, 6, widen_1, 0, unroll=True)
     near = jnp.abs(zo3 - 2 * zi3)
     pro_1 = jnp.where(near == 0, 1.0, jnp.where(near == 1, 0.5, 0.0)).astype(F32)
 
@@ -781,7 +781,7 @@
             x0[f, p] = x0[f, p] + keep[p] * v
         return carry
 
-    lax.fori_loop(0, 6, correct, 0)
+    lax.fori_loop(0, 6, correct, 0, unroll=True)
 
     def smooth_0(f, e, image):
         x0[f, e] = x0[f, e] + invd[e] * (b16[f, e] - image)
@@ -802,14 +802,14 @@
     line = iota((1, 128), 1)
 
     def energies(l, carry):
-        spread_planes(x0, 3 * l, 1, 5, m["g"], BZ, 2)
+        spread_planes(x0, 3 * l, 1, 5, m["g"].at[l], BZ, 2)
         curve = jnp.zeros((8, 128), F32)
         dot = jnp.zeros((8, 128), F32)
         for tile in range(2):
             q = pl.ds(128 * tile, 128)
             for e in range(4):
-                low = [m["g"][tile, e, k] for k in range(12)]
-                high = [m["g"][tile, e + 1, k] for k in range(12)]
+                low = [m["g"][l, tile, e, k] for k in range(12)]
+                high = [m["g"][l, tile, e + 1, k] for k in range(12)]
                 a = modes_of(low, high)
                 f = couple(a, None)
                 energy = None
@@ -827,7 +827,7 @@
             sums[...] = jnp.where(line == k, v, sums[...])
         return carry
 
-    lax.fori_loop(0, 2, energies, 0)
+    lax.fori_loop(0, 2, energies, 0, unroll=True)
 
     rc, sc, rx = m["rc"], m["sc"], m["rx"]
     twin = pltpu.make_async_remote_copy(
@@ -858,20 +858,18 @@
     twin.wait_recv()
     sc[...] = sums[...] + rc[...]
 
-    def tell(k, ax, ay):
-        pltpu.make_async_remote_copy(
-            src_ref=sc, dst_ref=rx.at[k], send_sem=group_send.at[3],
-            recv_sem=group_recv.at[3], device_id=(lax.rem(gx + ax, NX), lax.rem(gy + ay, NY)),
-            device_id_type=pl.DeviceIdType.MESH,
-        ).start()
-
-    def tell_far(k, carry):
-        tell(k, 1 + lax.rem(k // 4 + 13, NX - 1), 2 * lax.rem(k, 4))
-        return carry
-
-    lax.fori_loop(0, 4 * (NX - 1), tell_far, 0)
-    for k in range(3):
-        tell(4 * (NX - 1) + k, 0, 2 + 2 * k)
+    rows_of = [lax.rem(gy + 2 * k, NY) for k in range(4)]
+    k = 0
+    for ax in sorted(range(NX), key=lambda d: -min(d, NX - d)):
+        other = lax.rem(gx + ax, NX)
+        for j in (2, 1, 3, 0):
+            if (ax, j) != (0, 0):
+                pltpu.make_async_remote_copy(
+                    src_ref=sc, dst_ref=rx.at[k], send_sem=group_send.at[3],
+                    recv_sem=group_recv.at[3], device_id=(other, rows_of[j]),
+                    device_id_type=pl.DeviceIdType.MESH,
+                ).start()
+                k += 1
 
     for copy in fourth:
         copy.wait_recv()

time: 56 us -> 52.4 us (0.936)
  Pallas kernels: 55.3 us -> 51.6 us
    pallas_call x1, Pallas kernels: 53.6 us -> 50 us  [per_device(): pl.pallas_call(kernel, out_shape=(jax.ShapeDtypeStruct((2, 3, BX, BY, BZ)...]
where the time goes in v4:
time: 52.4 us; the launch traced here: 52.3 us
  Pallas kernels  51.6 us (98%)
  between operations  0.64 us (1%)
    pallas_call x1, Pallas kernels, per_device(): pl.pallas_call(kernel, out_shape=(jax.ShapeDtypeStruct((2, 3, BX, BY, BZ)...  50 us
    pallas_call x1, Pallas kernels, per_device(): pl.pallas_call(scale_kernel, out_shape=(jax.ShapeDtypeStruct((2, 3, BX, B...  1.65 us

profile of v4, /device:TPU:1, one launch (start us, length us, event | category | flops | bytes accessed | tf_op | source)
XLA Modules:
  0.0 52.3 jit_solution(15701993973801356599)
XLA Ops:
  0.6 50.0 %shard_map.76 = (f32[2,3,4,8,256]{4,3,2,1,0:T(8,128)}, f32[2,4,8,256]{3,2,1,0:T(8,128)}, f32[1,128]{1,0:T(1,128)}) custom-call(f32[4,8,256]{2,1,0:T(8,128)} %dens.1, s32[4,8,256]{2,1,0:T(8,128)} %pas_in.1, s32[4,8,256]{2,1,0:T(8,128)} %sup_in.1, s32[2,4,8,256]{3,2,1,0:T(8,128)} %lod_in.1, f32[2,3,4,8,256]{4,3,2,1,0:T(8,128)} %tra_in.1), custom_call_target="tpu_custom_call" | custom-call | tf_op jit(solution)/shard_map/pallas_call | solution.py:935
  50.6 1.7 %shard_map.77 = (f32[2,3,4,8,256]{4,3,2,1,0:T(8,128)}, f32[4,8,256]{2,1,0:T(8,128)}, f32[2]{0:T(128)}) custom-call(f32[2,3,4,8,256]{4,3,2,1,0:T(8,128)} %get-tuple-element.6.precond, f32[2,4,8,256]{3,2,1,0:T(8,128)} %get-tuple-element.7.filtered, f32[1,128]{1,0:T(1,128)} %get-tuple-element.8.scalars), custom_call_target="tpu_custom_call" | custom-call | tf_op jit(solution)/shard_map/pallas_call | solution.py:952

commit v5 on v4

--- a/solution.py
+++ b/solution.py
@@ -63,7 +63,12 @@
 
 
 def mm(a, b):
-    return jnp.dot(a, b, preferred_element_type=F32, precision=lax.Precision.HIGHEST)
+    b = b.astype(jnp.bfloat16)
+    high = a.astype(jnp.bfloat16)
+    low = (a - high.astype(F32)).astype(jnp.bfloat16)
+    return jnp.dot(high, b, preferred_element_type=F32) + jnp.dot(
+        low, b, preferred_element_type=F32
+    )
 
 
 def couple(a, s):
@@ -168,13 +173,13 @@
     lax.fori_loop(0, tiles, over_tile, 0, unroll=True)
 
 
-def gather_nodes(h_ref, e, c, z, lanes):
+def gather_nodes(h_ref, e, c, z, lanes, rows=16):
     def load(k):
-        rows = []
-        for half in range(2):
+        parts = []
+        for half in range(rows // 8):
             tiles = [h_ref[half * (lanes // 128) + q, e, 4 * c + k] for q in range(lanes // 128)]
-            rows.append(tiles[0] if len(tiles) == 1 else jnp.concatenate(tiles, axis=1))
-        return jnp.concatenate(rows, axis=0)
+            parts.append(tiles[0] if len(tiles) == 1 else jnp.concatenate(tiles, axis=1))
+        return parts[0] if len(parts) == 1 else jnp.concatenate(parts, axis=0)
 
     t = []
     for hz in range(2):
@@ -183,8 +188,10 @@
     return (t[0] - t[1]) + z_down(t[0] + t[1], z)
 
 
-def apply_level(x_ref, groups, xoff, s_ref, soff, scale, elements, g_ref, h_ref, z, lanes, use):
-    tiles = 2 * lanes // 128
+def apply_level(
+    x_ref, groups, xoff, s_ref, soff, scale, elements, g_ref, h_ref, z, lanes, use, rows=16
+):
+    tiles = rows // 8 * lanes // 128
 
     def one(l, carry):
         spread_planes(x_ref, 3 * l, xoff, elements + 1, g_ref.at[l], z, tiles)
@@ -192,7 +199,7 @@
 
         def nodes(e, inner):
             for c in range(3):
-                use(3 * l + c, e, gather_nodes(h_ref.at[l], e, c, z, lanes))
+                use(3 * l + c, e, gather_nodes(h_ref.at[l], e, c, z, lanes, rows))
             return inner
 
         lax.fori_loop(1, elements, nodes, 0, unroll=True)
@@ -201,24 +208,22 @@
     lax.fori_loop(0, groups, one, 0, unroll=True)
 
 
-def filter_plane(load, p):
-    a = [load(p), load(p - 1) + load(p + 1), load(p - 2) + load(p + 2)]
-    f = []
-    for c in range(3):
-        h = []
-        for b in range(3):
-            t = None
-            for i in range(3):
+def put_plane(ref, p, v):
+    ref[0, p] = v
+    ref[1, p] = y_up(v) + y_down(v)
+    ref[2, p] = y_up(v, 2) + y_down(v, 2)
+
+
+def filter_plane(ref, p, rows=16):
+    f = [None, None, None]
+    for b in range(3):
+        a = [ref[b, p, 0:rows]]
+        a += [ref[b, p - d, 0:rows] + ref[b, p + d, 0:rows] for d in (1, 2)]
+        for i in range(3):
+            for c in range(3):
                 w = weight(i, b, c)
                 if w > 0.0:
-                    t = w * a[i] if t is None else t + w * a[i]
-            h.append(t)
-        out = h[0]
-        if h[1] is not None:
-            out = out + (y_up(h[1]) + y_down(h[1]))
-        if h[2] is not None:
-            out = out + (y_up(h[2], 2) + y_down(h[2], 2))
-        f.append(out)
+                    f[c] = w * a[i] if f[c] is None else f[c] + w * a[i]
     z = f[0].shape[1]
     return (
         f[0]
@@ -232,7 +237,7 @@
     sup=(4, 8, BZ), lod=(2, 4, 8, BZ), tra=(2, 3, 4, 8, BZ), pas=(4, 8, BZ),
     ya_up=(4, 8, BZ), ya_dn=(4, 8, BZ), yb_up=(4, 8, BZ), yb_dn=(2, 4, 8, BZ),
     ra_lo=(12, 8, BZ), ra_hi=(12, 8, BZ), rb_lo=(7, 8, BZ), rb_hi=(2, 7, 8, BZ),
-    gden=(3, 16, BZ), d16=(12, 16, BZ), s16=(8, 16, BZ), coef=(8, 8, BZ),
+    gden=(3, 16, BZ), iden=(8, 16, BZ), d16=(3, 12, 16, BZ), s16=(8, 16, BZ), coef=(8, 8, BZ),
     b16=(6, 7, 16, BZ), x0=(6, 7, 16, BZ), keep=(7, 16, BZ), invd=(7, 16, BZ),
     g=(2, 4, 7, 12, 8, 128), h=(2, 4, 6, 12, 8, 128), r0=(6, 4, 8, BZ),
     zl=(18, 8, BZ), zr=(18, 8, 128), zc=(2, 8, 128),
@@ -241,14 +246,15 @@
     s1s=(2, 8, 128), rs1=(len(S1_SLOTS), 2, 8, 128),
     rp=(5, 4, 3, 8, 128), ru=(5, 3, 3, 8, 128), rd=(5, 3, 8, 128), re=(5, 3, 3, 8, 128),
     s1=(8, 16, 128), invd1=(7, 16, 128), b1=(6, 7, 16, 128), x1=(6, 7, 16, 128),
-    g1=(2, 2, 7, 12, 8, 128), h1=(2, 2, 6, 12, 8, 128), r1=(6, 3, 16, 128),
+    g1=(2, 2, 7, 12, 8, 128), h1=(2, 2, 6, 12, 8, 128), r1=(6, 3, 8, 128),
+    s1h=(5, 8, 128), invd1h=(5, 8, 128), b1h=(6, 5, 8, 128), x1h=(6, 5, 8, 128),
     t2l=(4, 8, BZ), t2r=(4, 8, 128), t2=(8, 128), t2v=(4, 8, 128), rb2=(len(R3_SLOTS), 8, 128),
     s2=(10, 16, 128), invd2=(10, 16, 128), b2=(3, 10, 16, 128), x2=(3, 10, 16, 128),
     g2=(1, 2, 10, 12, 8, 128), h2=(1, 2, 9, 12, 8, 128),
     yy2=(12, 16, 128), w2=(12, 16, BZ), yy1=(30, 16, 128), v1=(30, 16, BZ),
     sums=(1, 128), rc=(1, 128), sc=(1, 128), rx=(127, 1, 128),
     rt=(2, 8, 8, BZ), yt=(4, 8, BZ), rt_lo=(8, 8, BZ), rt_hi=(8, 8, BZ),
-    f16=(8, 16, BZ), fil=(2, 4, 8, BZ),
+    f16=(3, 8, 16, BZ), fil=(2, 4, 8, BZ),
 )
 INTS = ("sup", "lod", "pas")
 NAMES = list(SCRATCH)
@@ -324,6 +330,11 @@
             w = w if b == 0 else w * cy[b]
             total = w if total is None else total + w
         m["gden"][a] = total
+    for i in range(8):
+        x = gx * BX + i - 2
+        cx1 = in_x(x - 1, NX * BX) + in_x(x + 1, NX * BX)
+        cx2 = in_x(x - 2, NX * BX) + in_x(x + 2, NX * BX)
+        m["iden"][i] = 1.0 / (m["gden"][0] + cx1 * m["gden"][1] + cx2 * m["gden"][2])
 
     loads[1].wait()
     loads[0].wait()
@@ -357,26 +368,31 @@
     ra_lo, ra_hi, rb_lo, rb_hi = m["ra_lo"], m["ra_hi"], m["rb_lo"], m["rb_hi"]
     own = df.at[pl.ds(4, 4)]
     first = [
+        message(own, df.at[pl.ds(0, 4)], 1, 0),
+        message(own, df.at[pl.ds(8, 4)], -1, 0),
+        message(pf.at[pl.ds(4, 2)], pf.at[pl.ds(0, 2)], 1, 0),
+        message(pf.at[pl.ds(2, 2)], pf.at[pl.ds(6, 2)], -1, 0),
         message(m["ya_up"], ra_lo.at[pl.ds(0, 4)], 1, 1),
         message(m["ya_dn"], ra_hi.at[pl.ds(0, 4)], 1, -1),
         message(m["ya_up"], ra_lo.at[pl.ds(8, 4)], -1, 1),
         message(m["ya_dn"], ra_hi.at[pl.ds(8, 4)], -1, -1),
-        message(own, df.at[pl.ds(0, 4)], 1, 0),
-        message(own, df.at[pl.ds(8, 4)], -1, 0),
-        message(pf.at[pl.ds(4, 2)], pf.at[pl.ds(0, 2)], 1, 0),
-        message(pf.at[pl.ds(2, 2)], pf.at[pl.ds(6, 2)], -1, 0),
         message(m["ya_up"], ra_lo.at[pl.ds(4, 4)], 0, 1),
         message(m["ya_dn"], ra_hi.at[pl.ds(4, 4)], 0, -1),
     ]
     second = [
         message(m["yb_up"].at[pl.ds(3, 1)], rb_lo.at[pl.ds(0, 1)], 1, 1),
         message(m["yb_dn"].at[:, pl.ds(3, 1)], rb_hi.at[:, pl.ds(0, 1)], 1, -1),
-        message(m["yb_up"].at[pl.ds(0, 2)], rb_lo.at[pl.ds(5, 2)], -1, 1),
-        message(m["yb_dn"].at[:, pl.ds(0, 2)], rb_hi.at[:, pl.ds(5, 2)], -1, -1),
+        message(m["yb_up"].at[pl.ds(0, 1)], rb_lo.at[pl.ds(5, 1)], -1, 1),
+        message(m["yb_dn"].at[:, pl.ds(0, 1)], rb_hi.at[:, pl.ds(5, 1)], -1, -1),
         message(bf.at[:, pl.ds(4, 1)], bf.at[:, pl.ds(0, 1)], 1, 0),
-        message(bf.at[:, pl.ds(1, 2)], bf.at[:, pl.ds(5, 2)], -1, 0),
+        message(bf.at[:, pl.ds(1, 1)], bf.at[:, pl.ds(5, 1)], -1, 0),
         message(m["yb_up"], rb_lo.at[pl.ds(1, 4)], 0, 1),
         message(m["yb_dn"], rb_hi.at[:, pl.ds(1, 4)], 0, -1),
+    ]
+    last = [
+        message(m["yb_up"].at[pl.ds(1, 1)], rb_lo.at[pl.ds(6, 1)], -1, 1),
+        message(m["yb_dn"].at[:, pl.ds(1, 1)], rb_hi.at[:, pl.ds(6, 1)], -1, -1),
+        message(bf.at[:, pl.ds(2, 1)], bf.at[:, pl.ds(6, 1)], -1, 0),
     ]
     for copy in first + second:
         copy.start()
@@ -389,25 +405,22 @@
         halo = jnp.where(sub() < 4, ra_hi[p], ra_lo[p])
         both = jnp.concatenate([df[p], halo], axis=0)
         here = in_x(gx * BX + p - 4, NX * BX)
-        d16[p] = jnp.where(rows0 * here > 0.0, both, 0.0)
+        put_plane(d16, p, jnp.where(rows0 * here > 0.0, both, 0.0))
         return carry
 
     lax.fori_loop(0, 12, put_density, 0, unroll=True)
 
     def stiffen(i, carry):
         x = gx * BX + i - 2
-        number = filter_plane(lambda p: d16[p], i + 2)
-        cx1 = in_x(x - 1, NX * BX) + in_x(x + 1, NX * BX)
-        cx2 = in_x(x - 2, NX * BX) + in_x(x + 2, NX * BX)
-        denom = m["gden"][0] + cx1 * m["gden"][1] + cx2 * m["gden"][2]
-        level = jnp.tanh(8.0 * (number / denom - 0.5))
+        number = filter_plane(d16, i + 2)
+        level = jnp.tanh(8.0 * (number * m["iden"][i] - 0.5))
         slope = (1.0 - level * level) * (8.0 / (2.0 * EDGE))
         halo = pltpu.roll(jnp.where(sub() >= 4, ra_hi[i + 2], ra_lo[i + 2]), 4, 0)
         solid = jnp.concatenate([pf[i], halo], axis=0)
         phys = solid * ((EDGE + level) * (1.0 / (2.0 * EDGE)))
         stiff = 0.001 + 0.999 * (phys * phys * phys)
         s16[i] = jnp.where(rows0 * in_x(x, NX * BX) > 0.0, stiff, 0.0)
-        coef = -3.0 * 0.999 * (phys * phys) * solid * slope / denom
+        coef = -3.0 * 0.999 * (phys * phys) * solid * slope * m["iden"][i]
         m["coef"][i] = coef[0:8]
         return carry
 
@@ -437,6 +450,8 @@
 
     for copy in second:
         copy.wait_recv()
+    for copy in last:
+        copy.start()
     group(lambda dx, dy: m["s1s"], m["rs1"], S1_SLOTS, 0)
 
 
@@ -465,7 +480,7 @@
             x0[f, p] = inv * b
         return carry
 
-    lax.fori_loop(0, 7, begin, 0, unroll=True)
+    lax.fori_loop(0, 6, begin, 0, unroll=True)
 
     def residual(f, e, image):
         m["r0"][f, e - 1] = keep[e, 0:8] * (b16[f, e, 0:8] - image[0:8])
@@ -571,6 +586,11 @@
 
     lax.fori_loop(0, 7, diag1, 0, unroll=True)
 
+    s1h, invd1h = m["s1h"], m["invd1h"]
+    for p in range(5):
+        s1h[p] = jnp.where(sh < 5, s1[p, 0:8], s1[p, 8:16])
+        invd1h[p] = jnp.where(sh < 5, invd1[p, 0:8], invd1[p, 8:16])
+
     zi1, zo1 = iota((128, 128), 0), iota((128, 128), 1)
     pairs_2 = inside(zi1 // 2 == zo1 % 64) * 0.125
     t2l, t2r, t2 = m["t2l"], m["t2r"], m["t2"]
@@ -584,10 +604,13 @@
     t2r[3] = jnp.where(iota((8, 128), 1) < 64, w_own[0:8], dg[0:8])
     t2[6:8] = t2r[3, pl.ds(0, 2, stride=2)]
 
+    for copy in last:
+        copy.wait_recv()
+    begin(6, 0)
     for copy in third:
         copy.wait_recv()
 
-    b1, x1 = m["b1"], m["x1"]
+    b1, x1, b1h, x1h = m["b1"], m["x1"], m["b1h"], m["x1h"]
     okx = {d: (gx + d >= 0) & (gx + d < NX) for d in range(-2, 3)}
     oky = {d: (gy + d >= 0) & (gy + d < NY) for d in range(-1, 2)}
 
@@ -629,16 +652,21 @@
                         t0 = t0 + pb[f, x]
                     if mids[0] is not None:
                         t0 = t0 + mids[f]
-                    v = jnp.concatenate([t0, jnp.where(sh >= 6, up, 0.0)], axis=0)
-                    b1[f, p] = v
-                    x1[f, p] = invd1[p] * v
+                    t1 = jnp.where(sh >= 6, up, 0.0)
+                    if whole:
+                        v = jnp.concatenate([t0, t1], axis=0)
+                        b1[f, p] = v
+                        x1[f, p] = invd1[p] * v
+                    else:
+                        b1h[f, p] = t0 + t1
+                        x1h[f, p] = invd1h[p] * (t0 + t1)
 
     right_side_1(range(5), False)
 
     def residual_1(f, e, image):
-        m["r1"][f, e - 1] = b1[f, e] - image
-
-    apply_level(x1, 2, 0, s1, 1, 2.0, 4, m["g1"], m["h1"], 128, 128, residual_1)
+        m["r1"][f, e - 1] = b1h[f, e] - image
+
+    apply_level(x1h, 2, 0, s1h, 1, 2.0, 4, m["g1"], m["h1"], 128, 128, residual_1, 8)
 
     for c in range(3):
         sides = []
@@ -646,7 +674,7 @@
             r = [m["r1"][3 * l + c, x] for x in range(3)]
             v = r[1] + 0.5 * (r[0] + r[2])
             v = v + 0.5 * (y_up(v) + y_down(v))
-            sides.append(v[0:8])
+            sides.append(v)
         t2l[c] = jnp.concatenate(sides, axis=1)
     t2l[3] = jnp.zeros((8, BZ), F32)
     near = jnp.abs(zi2 % 128 - 2 * (zo2 % 64))
@@ -883,13 +911,13 @@
             halo = jnp.where((sub() >= 2) & (sub() < 6), 0.0, jnp.where(l == 0, plain, moved))
             both = jnp.concatenate([rt[l, p], halo], axis=0)
             here = rows0 * in_x(gx * BX + p - 2, NX * BX)
-            f16[p] = jnp.where(here > 0.0, both, 0.0)
+            put_plane(f16, p, jnp.where(here > 0.0, both, 0.0))
             return inner
 
         lax.fori_loop(0, 8, put, 0, unroll=True)
 
         def run(x, inner):
-            fil[l, x] = filter_plane(lambda p: f16[p], x + 2)[0:8]
+            fil[l, x] = filter_plane(f16, x + 2, 8)
             return inner
 
         lax.fori_loop(0, 4, run, 0, unroll=True)
@@ -911,7 +939,7 @@
     for copy in outs:
         copy.wait()
 
-    for copy in first + second + third + late + fourth:
+    for copy in first + second + last + third + late + fourth:
         copy.wait_send()
     group_done(m["rs1"], group_send, 0)
     group_done(rb2, group_send, 1)

time: 52.4 us -> 50.1 us (0.956)
  Pallas kernels: 51.6 us -> 49.3 us
    pallas_call x1, Pallas kernels: 50 us -> 47.7 us  [per_device(): pl.pallas_call(kernel, out_shape=(jax.ShapeDtypeStruct((2, 3, BX, BY, BZ)...]
where the time goes in v5:
time: 50.1 us; the launch traced here: 49.9 us
  Pallas kernels  49.3 us (98%)
  between operations  0.64 us (1%)
    pallas_call x1, Pallas kernels, per_device(): pl.pallas_call(kernel, out_shape=(jax.ShapeDtypeStruct((2, 3, BX, BY, BZ)...  47.7 us
    pallas_call x1, Pallas kernels, per_device(): pl.pallas_call(scale_kernel, out_shape=(jax.ShapeDtypeStruct((2, 3, BX, B...  1.65 us

profile of v5, /device:TPU:1, one launch (start us, length us, event | category | flops | bytes accessed | tf_op | source)
XLA Modules:
  0.0 49.9 jit_solution(11417060978855010149)
XLA Ops:
  0.6 47.7 %shard_map.76 = (f32[2,3,4,8,256]{4,3,2,1,0:T(8,128)}, f32[2,4,8,256]{3,2,1,0:T(8,128)}, f32[1,128]{1,0:T(1,128)}) custom-call(f32[4,8,256]{2,1,0:T(8,128)} %dens.1, s32[4,8,256]{2,1,0:T(8,128)} %pas_in.1, s32[4,8,256]{2,1,0:T(8,128)} %sup_in.1, s32[2,4,8,256]{3,2,1,0:T(8,128)} %lod_in.1, f32[2,3,4,8,256]{4,3,2,1,0:T(8,128)} %tra_in.1), custom_call_target="tpu_custom_call" | custom-call | tf_op jit(solution)/shard_map/pallas_call | solution.py:963
  48.3 1.7 %shard_map.77 = (f32[2,3,4,8,256]{4,3,2,1,0:T(8,128)}, f32[4,8,256]{2,1,0:T(8,128)}, f32[2]{0:T(128)}) custom-call(f32[2,3,4,8,256]{4,3,2,1,0:T(8,128)} %get-tuple-element.6.precond, f32[2,4,8,256]{3,2,1,0:T(8,128)} %get-tuple-element.7.filtered, f32[1,128]{1,0:T(1,128)} %get-tuple-element.8.scalars), custom_call_target="tpu_custom_call" | custom-call | tf_op jit(solution)/shard_map/pallas_call | solution.py:980
